TPU v7x, 256 devices: a whole 4x4x8 slice. The times are simulated.
256 devices in a mesh: gx: 16 (over x_lo, y, core), gy: 8 (over z), gz: 2 (over x_hi).
Axes of the slice: x: 4 (x_hi: 2, x_lo: 2; x = x_hi * 2 + x_lo), y: 4, z: 8, core: 2. Of those that a mesh axis runs over, the one named last changes fastest.
Arguments:
- fields: float32 [5, 2, 4096, 4096], P(None, 'gz', 'gx', 'gy'), parts along dimension 1, may hold values from -6 to 6
Outputs:
- deriv_x: float32 [5, 2, 4096, 4096], P(None, 'gz', 'gx', 'gy'), parts along dimension 1
- deriv_y: float32 [5, 2, 4096, 4096], P(None, 'gz', ('gx', 'gy')), parts along dimension 1
There are 2 independent parts, one for each index of `gz`. A program takes and returns all parts, laid end to end along the dimension named above; each array names one. Nothing has to cross between parts.
All inputs are finite; a program needn't handle non-finite values.
Results may differ from a plain program's by a relative error of at most 0.00002.
Values sent between devices are 32-bit elements; how exact they have to be, the bound alone decides.
No kernel may reach another device: no remote copies, remote signals or barrier semaphores. Data moves between devices by JAX's collectives and lax.ppermute only.
A program may use at most 64 MiB of HBM per device.

v0:
```python
import jax
import jax.numpy as jnp
from jax import lax
from jax.sharding import PartitionSpec as P

LEVELS = 4


def extended_2(cells, sides, width):
    for axis, dim in sides:
        count = lax.axis_size(axis)
        head = lax.slice_in_dim(cells, 0, width, axis=dim)
        tail = lax.slice_in_dim(cells, cells.shape[dim] - width, cells.shape[dim], axis=dim)
        cells = jnp.concatenate(
            [
                lax.ppermute(tail, axis, [(i, (i + 1) % count) for i in range(count)]),
                cells,
                lax.ppermute(head, axis, [((i + 1) % count, i) for i in range(count)]),
            ],
            axis=dim,
        )
    return cells


def coefficients(levels):
    upper = 1.0 / 3.0
    middle = 1.0
    factors = []
    for level in range(levels):
        factor = upper / middle
        factors.append(factor)
        middle = middle - 2.0 * factor * upper
        upper = -factor * upper
    return (factors, middle)


def right_side(field, axis):
    ahead = jnp.roll(field, -1, axis) - jnp.roll(field, 1, axis)
    farther = jnp.roll(field, -2, axis) - jnp.roll(field, 2, axis)
    return 7.0 / 9.0 * ahead + 1.0 / 36.0 * farther


def reduce_solve(values, axis):
    factors, middle = coefficients(LEVELS)
    for level in range(LEVELS):
        stride = 2**level
        values = values - factors[level] * (
            jnp.roll(values, stride, axis) + jnp.roll(values, -stride, axis)
        )
    return values / middle


def edge_stencil(extended):
    length = extended.shape[2]
    minus_two = lax.slice_in_dim(extended, 0, length - 4, axis=2)
    minus_one = lax.slice_in_dim(extended, 1, length - 3, axis=2)
    plus_one = lax.slice_in_dim(extended, 3, length - 1, axis=2)
    plus_two = lax.slice_in_dim(extended, 4, length, axis=2)
    return 7.0 / 9.0 * (plus_one - minus_one) + 1.0 / 36.0 * (plus_two - minus_two)


def body(fields):
    count = fields.shape[2]
    factors, middle = coefficients(LEVELS)
    bordered = extended_2(fields, (("gx", 2),), 2)
    values = edge_stencil(bordered)
    for level in range(LEVELS):
        stride = 2**level
        extended = extended_2(values, (("gx", 2),), stride)
        below = lax.slice_in_dim(extended, 0, count, axis=2)
        above = lax.slice_in_dim(extended, 2 * stride, 2 * stride + count, axis=2)
        values = values - factors[level] * (below + above)
    deriv_x = values / middle
    pencils = lax.all_to_all(fields, "gy", split_axis=2, concat_axis=3, tiled=True)
    deriv_y = reduce_solve(right_side(pencils, 3), 3)
    return (deriv_x, deriv_y)


def solution(mesh):
    placed = (P(None, "gz", "gx", "gy"),)
    return jax.shard_map(
        body,
        mesh=mesh,
        in_specs=placed,
        out_specs=(P(None, "gz", "gx", "gy"), P(None, "gz", ("gx", "gy"), None)),
        check_vma=False,
    )
```

profile of v0, /device:TPU:1, one launch (start us, length us, event | category | flops | bytes accessed | tf_op | source)
XLA Modules:
  0.0 129.2 jit_solution(3825977170244980457)
XLA Ops:
  0.6 5.4 %copy.12 = f32[5,1,256,512]{3,0,1,2:T(8,128)} copy(f32[5,1,256,512]{3,2,1,0:T(8,128)} %param.1) | data formatting | bytes 5242880 | tf_op args[0]
  6.0 9.3 %all-to-all-start = ((f32[5,1,256,512]{3,0,1,2:T(8,128)}), f32[5,1,256,512]{3,0,1,2:T(8,128)}, u32[]{:S(2)}, u32[]{:S(2)}) async-start(f32[5,1,256,512]{3,0,1,2:T(8,128)} %copy.12), calls=%async_computation | async-start | bytes 8388608 | tf_op jit(solution)/shard_map/all_to_all | solution.py:74
  15.3 1.0 collective-permute-start
  16.4 1.3 collective-permute-start.1
  17.9 1.1 collective-permute-done
  19.0 1.1 collective-permute-done.1
  20.1 1.1 fusion.3
  21.3 0.8 collective-permute-start.2
  22.1 4.0 %collective-permute-start.3 = (f32[5,1,1,512]{3,2,1,0:T(1,128)S(1)}, f32[5,1,1,512]{3,2,1,0:T(1,128)S(1)}, u32[]{:S(2)}, u32[]{:S(2)}) collective-permute-start(f32[5,1,1,512]{3,2,1,0:T(1,128)S(1)} %get-tuple-element.37), channel_id=1, source_target_pairs={{16,0},{32,16},{48,32},{64,48},{80,64},{96,80},{112,96},{128,112},... | collective-permute-start | bytes 30728 | tf_op jit(solution)/shard_map/ppermute | solution.py:18
  26.1 0.6 collective-permute-done.2
  26.9 0.6 fusion.16
  27.7 4.4 %collective-permute-start.5 = (f32[5,1,2,512]{3,2,1,0:T(2,128)S(1)}, f32[5,1,2,512]{3,2,1,0:T(2,128)S(1)}, u32[]{:S(2)}, u32[]{:S(2)}) collective-permute-start(f32[5,1,2,512]{3,2,1,0:T(2,128)S(1)} %get-tuple-element.35), channel_id=1, source_target_pairs={{16,0},{32,16},{48,32},{64,48},{80,64},{96,80},{112,96},{128,112},... | collective-permute-start | bytes 61448 | tf_op jit(solution)/shard_map/ppermute | solution.py:18
  32.1 0.6 collective-permute-done.4
  32.9 0.6 fusion.13
  33.6 4.9 %collective-permute-start.7 = (f32[5,1,4,512]{3,2,1,0:T(4,128)S(1)}, f32[5,1,4,512]{3,2,1,0:T(4,128)S(1)}, u32[]{:S(2)}, u32[]{:S(2)}) collective-permute-start(f32[5,1,4,512]{3,2,1,0:T(4,128)S(1)} %get-tuple-element.33), channel_id=1, source_target_pairs={{16,0},{32,16},{48,32},{64,48},{80,64},{96,80},{112,96},{128,112},... | collective-permute-start | bytes 122888 | tf_op jit(solution)/shard_map/ppermute | solution.py:18
  38.6 0.6 collective-permute-done.6
  40.3 5.1 %collective-permute-start.9 = (f32[5,1,8,512]{3,2,1,0:T(8,128)S(1)}, f32[5,1,8,512]{3,2,1,0:T(8,128)S(1)}, u32[]{:S(2)}, u32[]{:S(2)}) collective-permute-start(f32[5,1,8,512]{3,2,1,0:T(8,128)S(1)} %get-tuple-element.31), channel_id=1, source_target_pairs={{16,0},{32,16},{48,32},{64,48},{80,64},{96,80},{112,96},{128,112},... | collective-permute-start | bytes 245768 | tf_op jit(solution)/shard_map/ppermute | solution.py:18
  45.4 0.7 collective-permute-done.8
  46.3 1.9 %fusion.7 = f32[5,1,256,512]{3,2,1,0:T(8,128)} fusion(f32[5,1,256,512]{3,2,1,0:T(8,128)S(1)} %fusion.10, f32[5,1,8,512]{3,2,1,0:T(8,128)S(1)} %collective-permute-done.9, f32[5,1,8,512]{3,2,1,0:T(8,128)S(1)} %collective-permute-done.8), kind=kLoop, calls=%fused_computation.10 | loop fusion | flops 3932160 | bytes 5406720 | tf_op jit(solution)/shard_map/div | solution.py:73
  48.2 64.0 %all-to-all-done = f32[5,1,256,512]{3,0,1,2:T(8,128)} async-done(((f32[5,1,256,512]{3,0,1,2:T(8,128)}), f32[5,1,256,512]{3,0,1,2:T(8,128)}, u32[]{:S(2)}, u32[]{:S(2)}) %all-to-all-start) | async-done | bytes 2621472 | tf_op jit(solution)/shard_map/all_to_all | solution.py:74
  112.1 3.7 %copy.13 = f32[5,1,256,512]{3,2,0,1:T(8,128)S(1)} copy(f32[5,1,256,512]{3,0,1,2:T(8,128)} %all-to-all-done) | data formatting | bytes 5242880 | tf_op jit(solution)/shard_map/all_to_all | solution.py:74
  116.1 0.9 fusion.41
  117.0 0.9 fusion.43
  118.2 2.2 %fusion.20 = f32[5,1,32,4096]{3,2,0,1:T(8,128)S(1)} fusion(f32[5,1,32,1]{3,2,0,1:T(8,128)S(1)} %get-tuple-element.27, f32[5,1,32,4095]{3,2,0,1:T(8,128)S(1)} %get-tuple-element.29, f32[5,1,32,4095]{3,2,0,1:T(8,128)S(1)} %get-tuple-element.28, f32[5,1,32,1]{3,2,0,1:T(8,128)S(1)} %get-tuple-element.26, f32[5,1,32,2]{3,2,0,1:T(8,128)S(1)} %get-tuple-element.23, ...), kind=kLoop, calls=%fused_computation.32 | loop fusion | flops 5898240 | bytes 13107200 | tf_op jit(solution)/shard_map/add | solution.py:40
  120.4 0.9 fusion.38
  121.4 0.8 fusion.23
  122.2 0.9 fusion.36
  123.3 0.8 fusion.25
  124.0 0.9 fusion.34
  125.1 0.8 fusion.27
  125.9 0.9 fusion.32
  126.9 2.3 %fusion.31 = f32[5,1,32,4096]{3,2,1,0:T(8,128)} fusion(f32[5,1,32,4096]{3,2,0,1:T(8,128)S(1)} %fusion.27, f32[5,1,32,4088]{3,2,0,1:T(8,128)S(1)} %get-tuple-element.7, f32[5,1,32,8]{3,2,0,1:T(8,128)S(1)} %get-tuple-element.9, f32[5,1,32,8]{3,2,0,1:T(8,128)S(1)} %get-tuple-element.8, f32[5,1,32,4088]{3,2,0,1:T(8,128)S(1)} %get-tuple-element.6), kind=kLoop, calls=%fused_computation.48 | loop fusion | flops 3932160 | bytes 10485760
  (24 shorter events, 3.1 us)
Async XLA Ops:
  6.0 9.3 %copy-start = (f32[5,1,256,512]{3,2,1,0:T(8,128)S(1)}, f32[5,1,256,512]{3,2,1,0:T(8,128)}, u32[]{:S(2)}) copy-start(f32[5,1,256,512]{3,2,1,0:T(8,128)} %param.1) | copy-start | bytes 7864324
  6.0 106.1 %all-to-all-start = ((f32[5,1,256,512]{3,0,1,2:T(8,128)}), f32[5,1,256,512]{3,0,1,2:T(8,128)}, u32[]{:S(2)}, u32[]{:S(2)}) async-start(f32[5,1,256,512]{3,0,1,2:T(8,128)} %copy.12), calls=%async_computation | async-start | bytes 8388608 | tf_op jit(solution)/shard_map/all_to_all | solution.py:74
  15.3 3.7 %collective-permute-start = (f32[5,1,2,512]{3,2,1,0:T(2,128)S(1)}, f32[5,1,2,512]{3,2,1,0:T(2,128)S(1)}, u32[]{:S(2)}, u32[]{:S(2)}) collective-permute-start(f32[5,1,2,512]{3,2,1,0:T(2,128)S(1)} %get-tuple-element.38), channel_id=1, source_target_pairs={{16,0},{32,16},{48,32},{64,48},{80,64},{96,80},{112,96},{128,112},... | collective-permute-start | bytes 61448 | tf_op jit(solution)/shard_map/ppermute | solution.py:18
  16.4 3.8 %collective-permute-start.1 = (f32[5,1,2,512]{3,2,1,0:T(2,128)S(1)}, f32[5,1,2,512]{3,2,1,0:T(2,128)S(1)}, u32[]{:S(2)}, u32[]{:S(2)}) collective-permute-start(f32[5,1,2,512]{3,2,1,0:T(2,128)S(1)} %get-tuple-element.39), channel_id=1, source_target_pairs={{0,16},{16,32},{32,48},{48,64},{64,80},{80,96},{96,112},{112,128},... | collective-permute-start | bytes 61448 | tf_op jit(solution)/shard_map/ppermute | solution.py:16
  21.3 5.4 %collective-permute-start.2 = (f32[5,1,1,512]{3,2,1,0:T(1,128)S(1)}, f32[5,1,1,512]{3,2,1,0:T(1,128)S(1)}, u32[]{:S(2)}, u32[]{:S(2)}) collective-permute-start(f32[5,1,1,512]{3,2,1,0:T(1,128)S(1)} %get-tuple-element.36), channel_id=1, source_target_pairs={{0,16},{16,32},{32,48},{48,64},{64,80},{80,96},{96,112},{112,128},... | collective-permute-start | bytes 30728 | tf_op jit(solution)/shard_map/ppermute | solution.py:16
  22.1 4.9 %collective-permute-start.3 = (f32[5,1,1,512]{3,2,1,0:T(1,128)S(1)}, f32[5,1,1,512]{3,2,1,0:T(1,128)S(1)}, u32[]{:S(2)}, u32[]{:S(2)}) collective-permute-start(f32[5,1,1,512]{3,2,1,0:T(1,128)S(1)} %get-tuple-element.37), channel_id=1, source_target_pairs={{16,0},{32,16},{48,32},{64,48},{80,64},{96,80},{112,96},{128,112},... | collective-permute-start | bytes 30728 | tf_op jit(solution)/shard_map/ppermute | solution.py:18
  27.6 5.1 %collective-permute-start.4 = (f32[5,1,2,512]{3,2,1,0:T(2,128)S(1)}, f32[5,1,2,512]{3,2,1,0:T(2,128)S(1)}, u32[]{:S(2)}, u32[]{:S(2)}) collective-permute-start(f32[5,1,2,512]{3,2,1,0:T(2,128)S(1)} %get-tuple-element.34), channel_id=1, source_target_pairs={{0,16},{16,32},{32,48},{48,64},{64,80},{80,96},{96,112},{112,128},... | collective-permute-start | bytes 61448 | tf_op jit(solution)/shard_map/ppermute | solution.py:16
  27.7 5.2 %collective-permute-start.5 = (f32[5,1,2,512]{3,2,1,0:T(2,128)S(1)}, f32[5,1,2,512]{3,2,1,0:T(2,128)S(1)}, u32[]{:S(2)}, u32[]{:S(2)}) collective-permute-start(f32[5,1,2,512]{3,2,1,0:T(2,128)S(1)} %get-tuple-element.35), channel_id=1, source_target_pairs={{16,0},{32,16},{48,32},{64,48},{80,64},{96,80},{112,96},{128,112},... | collective-permute-start | bytes 61448 | tf_op jit(solution)/shard_map/ppermute | solution.py:18
  33.5 5.7 %collective-permute-start.6 = (f32[5,1,4,512]{3,2,1,0:T(4,128)S(1)}, f32[5,1,4,512]{3,2,1,0:T(4,128)S(1)}, u32[]{:S(2)}, u32[]{:S(2)}) collective-permute-start(f32[5,1,4,512]{3,2,1,0:T(4,128)S(1)} %get-tuple-element.32), channel_id=1, source_target_pairs={{0,16},{16,32},{32,48},{48,64},{64,80},{80,96},{96,112},{112,128},... | collective-permute-start | bytes 122888 | tf_op jit(solution)/shard_map/ppermute | solution.py:16
  33.6 5.8 %collective-permute-start.7 = (f32[5,1,4,512]{3,2,1,0:T(4,128)S(1)}, f32[5,1,4,512]{3,2,1,0:T(4,128)S(1)}, u32[]{:S(2)}, u32[]{:S(2)}) collective-permute-start(f32[5,1,4,512]{3,2,1,0:T(4,128)S(1)} %get-tuple-element.33), channel_id=1, source_target_pairs={{16,0},{32,16},{48,32},{64,48},{80,64},{96,80},{112,96},{128,112},... | collective-permute-start | bytes 122888 | tf_op jit(solution)/shard_map/ppermute | solution.py:18
  40.0 6.1 %collective-permute-start.8 = (f32[5,1,8,512]{3,2,1,0:T(8,128)S(1)}, f32[5,1,8,512]{3,2,1,0:T(8,128)S(1)}, u32[]{:S(2)}, u32[]{:S(2)}) collective-permute-start(f32[5,1,8,512]{3,2,1,0:T(8,128)S(1)} %get-tuple-element.30), channel_id=1, source_target_pairs={{0,16},{16,32},{32,48},{48,64},{64,80},{80,96},{96,112},{112,128},... | collective-permute-start | bytes 245768 | tf_op jit(solution)/shard_map/ppermute | solution.py:16
  40.3 6.0 %collective-permute-start.9 = (f32[5,1,8,512]{3,2,1,0:T(8,128)S(1)}, f32[5,1,8,512]{3,2,1,0:T(8,128)S(1)}, u32[]{:S(2)}, u32[]{:S(2)}) collective-permute-start(f32[5,1,8,512]{3,2,1,0:T(8,128)S(1)} %get-tuple-element.31), channel_id=1, source_target_pairs={{16,0},{32,16},{48,32},{64,48},{80,64},{96,80},{112,96},{128,112},... | collective-permute-start | bytes 245768 | tf_op jit(solution)/shard_map/ppermute | solution.py:18
where the time goes:
time: 129 us
  waiting for transfers between devices  69.7 us (54%)
  starting transfers between devices  31.3 us (24%)
  local copies, waits for them, and re-layouts  15.8 us (12%)
  other arithmetic  11.6 us (9%)
    all_to_all x1, waiting for transfers between devices, body(): lax.all_to_all(fields, 'gy', split_axis=2, concat_axis=3, tiled=True)  64 us
    ppermute x5, starting transfers between devices, extended_2(): lax.ppermute(head, axis, [((i + 1) % count, i) for i in range(count)])  19.5 us
    all_to_all x1, starting transfers between devices, body(): lax.all_to_all(fields, 'gy', split_axis=2, concat_axis=3, tiled=True)  9.28 us
    unnamed x4, local copies, waits for them, and re-layouts  5.67 us
    slice x8, local copies, waits for them, and re-layouts, reduce_solve(): jnp.roll(values, -stride, axis)  4.08 us
    all_to_all x2, local copies, waits for them, and re-layouts, body(): lax.all_to_all(fields, 'gy', split_axis=2, concat_axis=3, tiled=True)  3.95 us
    ppermute x5, waiting for transfers between devices, extended_2(): lax.ppermute(tail, axis, [(i, (i + 1) % count) for i in range(count)])  3.6 us
  transfers between devices with their start and end apart: 11, of which 11 were waited for; matrix products, arithmetic and copies ran while one was open for 4% of the time, Pallas kernels for 0%

commit v1 on v0

v1 whole, which is shorter than its diff:
```python
import jax
import jax.numpy as jnp
from jax import lax
from jax.experimental import pallas as pl
from jax.experimental.pallas import tpu as pltpu
from jax.sharding import PartitionSpec as P

LEVELS = 4
HALO = 24
LANES = 128
SUBLANES = 8
ORDER = (4, 3, 5, 2, 6, 1, 7)


def coefficients(levels):
    upper = 1.0 / 3.0
    middle = 1.0
    factors = []
    for level in range(levels):
        factor = upper / middle
        factors.append(factor)
        middle = middle - 2.0 * factor * upper
        upper = -factor * upper
    return (factors, middle)


def derivative(cells, axis):
    length = cells.shape[axis]

    def shifted(values, offset):
        return pltpu.roll(values, (-offset) % length, axis)

    factors, middle = coefficients(LEVELS)
    values = 7.0 / 9.0 * (shifted(cells, 1) - shifted(cells, -1)) + 1.0 / 36.0 * (
        shifted(cells, 2) - shifted(cells, -2)
    )
    for level in range(LEVELS):
        stride = 2**level
        values = values - factors[level] * (shifted(values, stride) + shifted(values, -stride))
    return values * (1.0 / middle)


def x_kernel(cells, below, above, out):
    fields, _, rows, columns = cells.shape
    tiles = columns // LANES

    def step(index, carry):
        field = index // tiles
        at = pl.ds(pl.multiple_of((index % tiles) * LANES, LANES), LANES)
        extended = jnp.concatenate(
            [below[field, 0, :, at], cells[field, 0, :, at], above[field, 0, :, at]], axis=0
        )
        out[field, 0, :, at] = derivative(extended, 0)[HALO : HALO + rows]
        return carry

    lax.fori_loop(0, fields * tiles, step, 0)


def y_kernel(*refs):
    parts = refs[:-3]
    out, result, sems = refs[-3:]
    count = len(parts)
    me = lax.axis_index("gy")
    fields, _, rows, columns = parts[0].shape
    groups = rows // SUBLANES

    def step(index, carry):
        field = index // groups
        at = pl.ds(pl.multiple_of((index % groups) * SUBLANES, SUBLANES), SUBLANES)
        row = jnp.concatenate([part[field, 0, at, :] for part in parts], axis=1)
        solved = derivative(row, 1)
        for part in range(count):
            column = pl.multiple_of(lax.rem(me + part, count) * columns, columns)
            result[field, 0, at, pl.ds(column, columns)] = solved[:, part * columns : (part + 1) * columns]
        return carry

    copies = []
    for field in range(fields):
        lax.fori_loop(field * groups, (field + 1) * groups, step, 0)
        copy = pltpu.make_async_copy(result.at[field], out.at[field], sems.at[field])
        copy.start()
        copies.append(copy)
    for copy in copies:
        copy.wait()


def body(fields):
    count = lax.axis_size("gy")
    ring = lax.axis_size("gx")
    me = lax.axis_index("gy")
    depth, slab, rows, columns = fields.shape
    part = rows // count

    def block(owner):
        return lax.dynamic_slice_in_dim(fields, lax.rem(owner, count) * part, part, 2)

    parts = [block(me)] + [None] * (count - 1)
    for hop in ORDER:
        parts[count - hop] = lax.ppermute(
            block(me + hop), "gy", [(i, (i + hop) % count) for i in range(count)]
        )
    below = lax.ppermute(fields[:, :, rows - HALO :], "gx", [(i, (i + 1) % ring) for i in range(ring)])
    above = lax.ppermute(fields[:, :, :HALO], "gx", [((i + 1) % ring, i) for i in range(ring)])
    vmem = pl.BlockSpec(memory_space=pltpu.VMEM)
    deriv_x = pl.pallas_call(
        x_kernel,
        out_shape=jax.ShapeDtypeStruct(fields.shape, fields.dtype),
        in_specs=[vmem] * 3,
        out_specs=vmem,
        cost_estimate=pl.CostEstimate(
            flops=20 * fields.size, bytes_accessed=8 * fields.size, transcendentals=0
        ),
    )(fields, below, above)
    deriv_y = pl.pallas_call(
        y_kernel,
        out_shape=jax.ShapeDtypeStruct((depth, slab, part, count * columns), fields.dtype),
        in_specs=[vmem] * count,
        out_specs=pl.BlockSpec(memory_space=pl.ANY),
        scratch_shapes=[
            pltpu.VMEM((depth, slab, part, count * columns), jnp.float32),
            pltpu.SemaphoreType.DMA((depth,)),
        ],
        cost_estimate=pl.CostEstimate(
            flops=20 * fields.size, bytes_accessed=8 * fields.size, transcendentals=0
        ),
    )(*parts)
    return (deriv_x, deriv_y)


def solution(mesh):
    placed = (P(None, "gz", "gx", "gy"),)
    return jax.shard_map(
        body,
        mesh=mesh,
        in_specs=placed,
        out_specs=(P(None, "gz", "gx", "gy"), P(None, "gz", ("gx", "gy"), None)),
        check_vma=False,
    )
```

time: 129 us -> 96.2 us (0.75)
  Pallas kernels: 0 us -> 23.7 us
  waiting for transfers between devices: 69.7 us -> 51.7 us
  starting transfers between devices: 31.3 us -> 15.4 us
  other arithmetic: 11.6 us -> 0 us
  local copies, waits for them, and re-layouts: 15.8 us -> 4.52 us
    all_to_all x1 -> x0, waiting for transfers between devices: 64 us -> none  [body(): lax.all_to_all(fields, 'gy', split_axis=2, concat_axis=3, tiled=True)]
    ppermute x10 -> x9, waiting for transfers between devices: 5.68 us -> 51.7 us  [the longest x7 47.7 us: body(): lax.ppermute(block(me + hop), 'gy', [(i, (i + hop) % count) for i in rang...]
    pallas_call x0 -> x2, Pallas kernels: none -> 23.7 us  [the longest x1 16.4 us: body(): pl.pallas_call(y_kernel, out_shape=jax.ShapeDtypeStruct((depth, slab, par...]
    all_to_all x1 -> x0, starting transfers between devices: 9.28 us -> none  [body(): lax.all_to_all(fields, 'gy', split_axis=2, concat_axis=3, tiled=True)]
    ppermute x10 -> x9, starting transfers between devices: 22 us -> 15.4 us  [the longest x7 12.9 us: body(): lax.ppermute(block(me + hop), 'gy', [(i, (i + hop) % count) for i in rang...]
    slice x17 -> x1, local copies, waits for them, and re-layouts: 6.22 us -> 1.1 us  [body(): fields[:, :, :HALO]]
    unnamed x4 -> x14, local copies, waits for them, and re-layouts: 5.67 us -> 0.71 us
    sub x6 -> x0, other arithmetic: 4.07 us -> none  [the longest x3 2.33 us: reduce_solve(): values - factors[level] * (jnp.roll(values, stride, axis) + jnp.roll(valu...]
  transfers between devices with their start and end apart: 11 -> 9, of which waited for: 11 -> 5; matrix products, arithmetic and copies ran while one was open for 4% -> 1% of each run, Pallas kernels for 0% -> 8%
where the time goes in v1:
time: 96.2 us; the launch traced here: 96 us
  waiting for transfers between devices  51.7 us (54%)
  Pallas kernels  23.7 us (25%)
  starting transfers between devices  15.4 us (16%)
  local copies, waits for them, and re-layouts  4.52 us (5%)
    ppermute x7, waiting for transfers between devices, body(): lax.ppermute(block(me + hop), 'gy', [(i, (i + hop) % count) for i in rang...  47.7 us
    pallas_call x1, Pallas kernels, body(): pl.pallas_call(y_kernel, out_shape=jax.ShapeDtypeStruct((depth, slab, par...  16.4 us
    ppermute x7, starting transfers between devices, body(): lax.ppermute(block(me + hop), 'gy', [(i, (i + hop) % count) for i in rang...  12.9 us
    pallas_call x1, Pallas kernels, body(): pl.pallas_call(x_kernel, out_shape=jax.ShapeDtypeStruct(fields.shape, fie...  7.31 us
    ppermute x1, waiting for transfers between devices, body(): lax.ppermute(fields[:, :, rows - HALO:], 'gx', [(i, (i + 1) % ring) for i...  2.97 us
    dynamic_slice x1, local copies, waits for them, and re-layouts, block(): lax.dynamic_slice_in_dim(fields, lax.rem(owner, count) * part, part, 2)  2.72 us
    ppermute x1, starting transfers between devices, body(): lax.ppermute(fields[:, :, rows - HALO:], 'gx', [(i, (i + 1) % ring) for i...  2.49 us
  transfers between devices with their start and end apart: 9, of which 5 were waited for; matrix products, arithmetic and copies ran while one was open for 1% of the time, Pallas kernels for 8%

profile of v1, /device:TPU:1, one launch (start us, length us, event | category | flops | bytes accessed | tf_op | source)
XLA Modules:
  0.0 96.0 jit_solution(11896830001373463356)
XLA Ops:
  0.7 2.7 %constant_dynamic-slice_fusion = (f32[5,1,32,512]{3,2,1,0:T(8,128)S(1)}, f32[5,1,32,512]{3,2,1,0:T(8,128)S(1)}, f32[5,1,32,512]{3,2,1,0:T(8,128)S(1)}, f32[5,1,3...) fusion(f32[5,1,256,512]{3,2,1,0:T(8,128)} %cells.1, ...), kind=kLoop, calls=%fused_computation | loop fusion | bytes 5242912 | tf_op jit(solution)/shard_map/dynamic_slice | solution.py:95
  3.4 6.4 %collective-permute-start.2 = (f32[5,1,32,512]{3,2,1,0:T(8,128)S(1)}, f32[5,1,32,512]{3,2,1,0:T(8,128)S(1)}, u32[]{:S(2)}, u32[]{:S(2)}) collective-permute-start(f32[5,1,32,512]{3,2,1,0:T(8,128)S(1)} %get-tuple-element.7), channel_id=1, source_target_pairs={{0,14},{2,0},{4,2},{6,4},{8,6},{10,8},{12,10},{14,12},{1,15},{3,1}... | collective-permute-start | bytes 983048 | tf_op jit(solution)/shard_map/ppermute | solution.py:99
  9.8 1.2 %collective-permute-start.3 = (f32[5,1,32,512]{3,2,1,0:T(8,128)S(1)}, f32[5,1,32,512]{3,2,1,0:T(8,128)S(1)}, u32[]{:S(2)}, u32[]{:S(2)}) collective-permute-start(f32[5,1,32,512]{3,2,1,0:T(8,128)S(1)} %get-tuple-element.6), channel_id=1, source_target_pairs={{0,12},{2,14},{4,0},{6,2},{8,4},{10,6},{12,8},{14,10},{1,13},{3,15... | collective-permute-start | bytes 983048 | tf_op jit(solution)/shard_map/ppermute | solution.py:99
  11.0 1.1 %fusion = (f32[5,1,24,512]{3,2,1,0:T(8,128)S(1)}, f32[5,1,24,512]{3,2,1,0:T(8,128)S(1)}) fusion(f32[5,1,256,512]{3,2,1,0:T(8,128)} %cells.1), kind=kLoop, calls=%fused_computation.8 | loop fusion | bytes 983040 | tf_op jit(solution)/shard_map/slice | solution.py:103
  12.1 2.5 %collective-permute-start = (f32[5,1,24,512]{3,2,1,0:T(8,128)S(1)}, f32[5,1,24,512]{3,2,1,0:T(8,128)S(1)}, u32[]{:S(2)}, u32[]{:S(2)}) collective-permute-start(f32[5,1,24,512]{3,2,1,0:T(8,128)S(1)} %get-tuple-element.11), channel_id=1, source_target_pairs={{0,16},{16,32},{32,48},{48,64},{64,80},{80,96},{96,112},{112,128},... | collective-permute-start | bytes 737288 | tf_op jit(solution)/shard_map/ppermute | solution.py:102
  14.6 0.0 collective-permute-start.1
  14.6 0.2 collective-permute-start.4
  14.7 3.0 %collective-permute-done.below = f32[5,1,24,512]{3,2,1,0:T(8,128)S(1)} collective-permute-done((f32[5,1,24,512]{3,2,1,0:T(8,128)S(1)}, f32[5,1,24,512]{3,2,1,0:T(8,128)S(1)}, u32[]{:S(2)}, u32[]{:S(2)}) %collective-permute-start) | collective-permute-done | bytes 245792 | tf_op jit(solution)/shard_map/ppermute | solution.py:102
  17.7 0.0 copy-start.5
  17.7 1.8 %collective-permute-start.5 = (f32[5,1,32,512]{3,2,1,0:T(8,128)S(1)}, f32[5,1,32,512]{3,2,1,0:T(8,128)S(1)}, u32[]{:S(2)}, u32[]{:S(2)}) collective-permute-start(f32[5,1,32,512]{3,2,1,0:T(8,128)S(1)} %get-tuple-element.4), channel_id=1, source_target_pairs={{0,8},{2,10},{4,12},{6,14},{8,0},{10,2},{12,4},{14,6},{1,9},{3,11}... | collective-permute-start | bytes 983048 | tf_op jit(solution)/shard_map/ppermute | solution.py:99
  19.5 1.0 %collective-permute-done.1.above = f32[5,1,24,512]{3,2,1,0:T(8,128)S(1)} collective-permute-done((f32[5,1,24,512]{3,2,1,0:T(8,128)S(1)}, f32[5,1,24,512]{3,2,1,0:T(8,128)S(1)}, u32[]{:S(2)}, u32[]{:S(2)}) %collective-permute-start.1) | collective-permute-done | bytes 245792 | tf_op jit(solution)/shard_map/ppermute | solution.py:103
  20.5 0.0 copy-start.6
  20.5 0.7 copy-done.6
  21.2 0.9 collective-permute-start.6
  22.1 0.0 collective-permute-done.2.refs_1_
  22.1 2.4 %collective-permute-start.7 = (f32[5,1,32,512]{3,2,1,0:T(8,128)S(1)}, f32[5,1,32,512]{3,2,1,0:T(8,128)}, u32[]{:S(2)}, u32[]{:S(2)}) collective-permute-start(f32[5,1,32,512]{3,2,1,0:T(8,128)S(1)} %get-tuple-element.9), channel_id=1, source_target_pairs={{0,4},{2,6},{4,8},{6,10},{8,12},{10,14},{12,0},{14,2},{1,5},{3,7},... | collective-permute-start | bytes 983048 | tf_op jit(solution)/shard_map/ppermute | solution.py:99
  24.5 12.1 %collective-permute-done.3.refs_2_ = f32[5,1,32,512]{3,2,1,0:T(8,128)S(1)} collective-permute-done((f32[5,1,32,512]{3,2,1,0:T(8,128)S(1)}, f32[5,1,32,512]{3,2,1,0:T(8,128)S(1)}, u32[]{:S(2)}, u32[]{:S(2)}) %collective-permute-start.3) | collective-permute-done | bytes 327712 | tf_op jit(solution)/shard_map/ppermute | solution.py:99
  36.6 0.0 collective-permute-start.8
  36.6 0.0 copy-done.5
  36.6 7.3 %shard_map.30 = f32[5,1,256,512]{3,2,1,0:T(8,128)} custom-call(f32[5,1,256,512]{3,2,1,0:T(8,128)} %cells.1, f32[5,1,24,512]{3,2,1,0:T(8,128)} %copy-done.5, f32[5,1,24,512]{3,2,1,0:T(8,128)} %copy-done.6), custom_call_target="tpu_custom_call" | custom-call | flops 13107200 | bytes 5242880 | tf_op jit(solution)/shard_map/pallas_call | solution.py:105
  44.0 0.0 copy-done
  44.0 0.0 copy-done.1
  44.0 21.4 %collective-permute-done.4.refs_3_ = f32[5,1,32,512]{3,2,1,0:T(8,128)S(1)} collective-permute-done((f32[5,1,32,512]{3,2,1,0:T(8,128)S(1)}, f32[5,1,32,512]{3,2,1,0:T(8,128)S(1)}, u32[]{:S(2)}, u32[]{:S(2)}) %collective-permute-start.4) | collective-permute-done | bytes 327712 | tf_op jit(solution)/shard_map/ppermute | solution.py:99
  65.3 0.0 collective-permute-done.5.refs_4_
  65.3 0.0 collective-permute-done.6.refs_5_
  65.3 0.0 copy-start.4
  65.4 0.0 collective-permute-done.7.refs_6_
  65.4 14.3 %collective-permute-done.8.refs_7_ = f32[5,1,32,512]{3,2,1,0:T(8,128)} collective-permute-done((f32[5,1,32,512]{3,2,1,0:T(8,128)S(1)}, f32[5,1,32,512]{3,2,1,0:T(8,128)}, u32[]{:S(2)}, u32[]{:S(2)}) %collective-permute-start.8) | collective-permute-done | bytes 327712 | tf_op jit(solution)/shard_map/ppermute | solution.py:99
  79.6 0.0 copy-done.2
  79.6 0.0 copy-done.3
  79.6 0.0 copy-done.4
  79.6 16.4 %shard_map.31 = f32[5,1,32,4096]{3,2,1,0:T(8,128)} custom-call(f32[5,1,32,512]{3,2,1,0:T(8,128)} %get-tuple-element.8.refs_0_, f32[5,1,32,512]{3,2,1,0:T(8,128)} %copy-done, f32[5,1,32,512]{3,2,1,0:T(8,128)} %copy-done.1, f32[5,1,32,512]{3,2,1,0:T(8,128)} %copy-done.2, f32[5,1,32,512]{3,2,1,0:T(8,128)} %copy-done.3, f32[5,1,32,512]{3,2,1,0:T(8,128)} %copy-done.4, ...), custom_call_target="tpu_custom_call" | custom-call | flops 13107200 | bytes 5242880 | tf_op jit(solution)/shard_map/pallas_call | solution.py:114
  (4 shorter events, 0.0 us)
Async XLA Ops:
  3.4 18.7 %collective-permute-start.2 = (f32[5,1,32,512]{3,2,1,0:T(8,128)S(1)}, f32[5,1,32,512]{3,2,1,0:T(8,128)S(1)}, u32[]{:S(2)}, u32[]{:S(2)}) collective-permute-start(f32[5,1,32,512]{3,2,1,0:T(8,128)S(1)} %get-tuple-element.7), channel_id=1, source_target_pairs={{0,14},{2,0},{4,2},{6,4},{8,6},{10,8},{12,10},{14,12},{1,15},{3,1}... | collective-permute-start | bytes 983048 | tf_op jit(solution)/shard_map/ppermute | solution.py:99
  9.8 26.8 %collective-permute-start.3 = (f32[5,1,32,512]{3,2,1,0:T(8,128)S(1)}, f32[5,1,32,512]{3,2,1,0:T(8,128)S(1)}, u32[]{:S(2)}, u32[]{:S(2)}) collective-permute-start(f32[5,1,32,512]{3,2,1,0:T(8,128)S(1)} %get-tuple-element.6), channel_id=1, source_target_pairs={{0,12},{2,14},{4,0},{6,2},{8,4},{10,6},{12,8},{14,10},{1,13},{3,15... | collective-permute-start | bytes 983048 | tf_op jit(solution)/shard_map/ppermute | solution.py:99
  12.1 5.6 %collective-permute-start = (f32[5,1,24,512]{3,2,1,0:T(8,128)S(1)}, f32[5,1,24,512]{3,2,1,0:T(8,128)S(1)}, u32[]{:S(2)}, u32[]{:S(2)}) collective-permute-start(f32[5,1,24,512]{3,2,1,0:T(8,128)S(1)} %get-tuple-element.11), channel_id=1, source_target_pairs={{0,16},{16,32},{32,48},{48,64},{64,80},{80,96},{96,112},{112,128},... | collective-permute-start | bytes 737288 | tf_op jit(solution)/shard_map/ppermute | solution.py:102
  14.6 5.9 %collective-permute-start.1 = (f32[5,1,24,512]{3,2,1,0:T(8,128)S(1)}, f32[5,1,24,512]{3,2,1,0:T(8,128)S(1)}, u32[]{:S(2)}, u32[]{:S(2)}) collective-permute-start(f32[5,1,24,512]{3,2,1,0:T(8,128)S(1)} %get-tuple-element.10), channel_id=1, source_target_pairs={{16,0},{32,16},{48,32},{64,48},{80,64},{96,80},{112,96},{128,112},... | collective-permute-start | bytes 737288 | tf_op jit(solution)/shard_map/ppermute | solution.py:103
  14.6 50.8 %collective-permute-start.4 = (f32[5,1,32,512]{3,2,1,0:T(8,128)S(1)}, f32[5,1,32,512]{3,2,1,0:T(8,128)S(1)}, u32[]{:S(2)}, u32[]{:S(2)}) collective-permute-start(f32[5,1,32,512]{3,2,1,0:T(8,128)S(1)} %get-tuple-element.5), channel_id=1, source_target_pairs={{0,10},{2,12},{4,14},{6,0},{8,2},{10,4},{12,6},{14,8},{1,11},{3,13... | collective-permute-start | bytes 983048 | tf_op jit(solution)/shard_map/ppermute | solution.py:99
  17.7 18.9 %copy-start.5 = (f32[5,1,24,512]{3,2,1,0:T(8,128)}, f32[5,1,24,512]{3,2,1,0:T(8,128)S(1)}, u32[]{:S(2)}) copy-start(f32[5,1,24,512]{3,2,1,0:T(8,128)S(1)} %collective-permute-done.below) | copy-start | bytes 737284
  17.7 47.6 %collective-permute-start.5 = (f32[5,1,32,512]{3,2,1,0:T(8,128)S(1)}, f32[5,1,32,512]{3,2,1,0:T(8,128)S(1)}, u32[]{:S(2)}, u32[]{:S(2)}) collective-permute-start(f32[5,1,32,512]{3,2,1,0:T(8,128)S(1)} %get-tuple-element.4), channel_id=1, source_target_pairs={{0,8},{2,10},{4,12},{6,14},{8,0},{10,2},{12,4},{14,6},{1,9},{3,11}... | collective-permute-start | bytes 983048 | tf_op jit(solution)/shard_map/ppermute | solution.py:99
  20.5 0.7 copy-start.6
  21.2 44.2 %collective-permute-start.6 = (f32[5,1,32,512]{3,2,1,0:T(8,128)S(1)}, f32[5,1,32,512]{3,2,1,0:T(8,128)S(1)}, u32[]{:S(2)}, u32[]{:S(2)}) collective-permute-start(f32[5,1,32,512]{3,2,1,0:T(8,128)S(1)} %get-tuple-element.3), channel_id=1, source_target_pairs={{0,6},{2,8},{4,10},{6,12},{8,14},{10,0},{12,2},{14,4},{1,7},{3,9},... | collective-permute-start | bytes 983048 | tf_op jit(solution)/shard_map/ppermute | solution.py:99
  22.1 21.8 %copy-start = (f32[5,1,32,512]{3,2,1,0:T(8,128)}, f32[5,1,32,512]{3,2,1,0:T(8,128)S(1)}, u32[]{:S(2)}) copy-start(f32[5,1,32,512]{3,2,1,0:T(8,128)S(1)} %collective-permute-done.2.refs_1_) | copy-start | bytes 983044
  22.1 43.2 %collective-permute-start.7 = (f32[5,1,32,512]{3,2,1,0:T(8,128)S(1)}, f32[5,1,32,512]{3,2,1,0:T(8,128)}, u32[]{:S(2)}, u32[]{:S(2)}) collective-permute-start(f32[5,1,32,512]{3,2,1,0:T(8,128)S(1)} %get-tuple-element.9), channel_id=1, source_target_pairs={{0,4},{2,6},{4,8},{6,10},{8,12},{10,14},{12,0},{14,2},{1,5},{3,7},... | collective-permute-start | bytes 983048 | tf_op jit(solution)/shard_map/ppermute | solution.py:99
  36.6 7.3 %copy-start.1 = (f32[5,1,32,512]{3,2,1,0:T(8,128)}, f32[5,1,32,512]{3,2,1,0:T(8,128)S(1)}, u32[]{:S(2)}) copy-start(f32[5,1,32,512]{3,2,1,0:T(8,128)S(1)} %collective-permute-done.3.refs_2_) | copy-start | bytes 983044
  36.6 43.0 %collective-permute-start.8 = (f32[5,1,32,512]{3,2,1,0:T(8,128)S(1)}, f32[5,1,32,512]{3,2,1,0:T(8,128)}, u32[]{:S(2)}, u32[]{:S(2)}) collective-permute-start(f32[5,1,32,512]{3,2,1,0:T(8,128)S(1)} %get-tuple-element.2), channel_id=1, source_target_pairs={{0,2},{2,4},{4,6},{6,8},{8,10},{10,12},{12,14},{14,0},{1,3},{3,5},... | collective-permute-start | bytes 983048 | tf_op jit(solution)/shard_map/ppermute | solution.py:99
  65.3 14.3 %copy-start.2 = (f32[5,1,32,512]{3,2,1,0:T(8,128)}, f32[5,1,32,512]{3,2,1,0:T(8,128)S(1)}, u32[]{:S(2)}) copy-start(f32[5,1,32,512]{3,2,1,0:T(8,128)S(1)} %collective-permute-done.4.refs_3_) | copy-start | bytes 983044
  65.3 14.3 %copy-start.3 = (f32[5,1,32,512]{3,2,1,0:T(8,128)}, f32[5,1,32,512]{3,2,1,0:T(8,128)S(1)}, u32[]{:S(2)}) copy-start(f32[5,1,32,512]{3,2,1,0:T(8,128)S(1)} %collective-permute-done.5.refs_4_) | copy-start | bytes 983044
  65.3 14.3 %copy-start.4 = (f32[5,1,32,512]{3,2,1,0:T(8,128)}, f32[5,1,32,512]{3,2,1,0:T(8,128)S(1)}, u32[]{:S(2)}) copy-start(f32[5,1,32,512]{3,2,1,0:T(8,128)S(1)} %collective-permute-done.6.refs_5_) | copy-start | bytes 983044

commit v2 on v1

v2 whole, which is shorter than its diff:
```python
import jax
import jax.numpy as jnp
import numpy as np
from jax import lax
from jax.experimental import pallas as pl
from jax.experimental.pallas import tpu as pltpu
from jax.sharding import PartitionSpec as P

LEVELS = 4
HALO = 24
LIMIT = 16 * 2**20
STEPS = (
    ("y4", ()),
    ("b", ()),
    ("a", ()),
    ("X", ()),
    ("y3", ()),
    ("y5", ()),
    ("y2", ("y4", "b", )),
    ("y6", ("y4", "a", )),
    ("y1", ("y3", "X", )),
    ("y7", ("y5", )),
    ("A", ()),
    ("B", ()),
    ("C", ()),
)
GROUPS = ((4,), (3, 5), (2, 6, 1, 7, 0))
LANES = 128
UNIT = 256
REACH = 17


def coefficients(levels):
    upper = 1.0 / 3.0
    middle = 1.0
    factors = []
    for level in range(levels):
        factor = upper / middle
        factors.append(factor)
        middle = middle - 2.0 * factor * upper
        upper = -factor * upper
    return (factors, middle)


def band():
    taps = np.zeros(2 * REACH + 1)
    for offset, weight in ((1, 7.0 / 9.0), (2, 1.0 / 36.0)):
        taps[REACH + offset] = weight
        taps[REACH - offset] = -weight
    factors, middle = coefficients(LEVELS)
    for level in range(LEVELS):
        stride = 2**level
        last = taps
        taps = last.copy()
        taps[stride:] -= factors[level] * last[:-stride]
        taps[:-stride] -= factors[level] * last[stride:]
    matrix = np.zeros((UNIT + 2 * LANES, UNIT))
    for column in range(UNIT):
        first = LANES + column - REACH
        matrix[first : first + 2 * REACH + 1, column] = taps / middle
    return matrix.astype(np.float32)


def derivative(cells, axis):
    length = cells.shape[axis]

    def shifted(values, offset):
        return pltpu.roll(values, (-offset) % length, axis)

    factors, middle = coefficients(LEVELS)
    values = 7.0 / 9.0 * (shifted(cells, 1) - shifted(cells, -1)) + 1.0 / 36.0 * (
        shifted(cells, 2) - shifted(cells, -2)
    )
    for level in range(LEVELS):
        stride = 2**level
        values = values - factors[level] * (shifted(values, stride) + shifted(values, -stride))
    return values * (1.0 / middle)


def x_kernel(cells, below, above, out):
    fields, _, rows, columns = cells.shape
    tiles = columns // LANES

    def step(index, carry):
        field = index // tiles
        at = pl.ds(pl.multiple_of((index % tiles) * LANES, LANES), LANES)
        extended = jnp.concatenate(
            [below[field, 0, :, at], cells[field, 0, :, at], above[field, 0, :, at]], axis=0
        )
        out[field, 0, :, at] = derivative(extended, 0)[HALO : HALO + rows]
        return carry

    lax.fori_loop(0, fields * tiles, step, 0)


def cut_kernel(count, hops, chunks):
    def kernel(fields, *refs):
        outs, sems = refs[:-1], refs[-1]
        me = lax.axis_index("gy")
        copies = []
        for first, last in chunks:
            for hop in hops:
                rows = outs[len(copies)].shape[2]
                at = pl.multiple_of(lax.rem(me + hop, count) * rows, rows)
                copy = pltpu.make_async_copy(
                    fields.at[first:last, :, pl.ds(at, rows), :], outs[len(copies)], sems.at[len(copies)]
                )
                copy.start()
                copies.append(copy)
        for copy in copies:
            copy.wait()

    return kernel


def terms(values):
    high = values.astype(jnp.bfloat16)
    rest = values - high.astype(jnp.float32)
    middle = rest.astype(jnp.bfloat16)
    low = (rest - middle.astype(jnp.float32)).astype(jnp.bfloat16)
    return (high, middle, low)


def product(one, other, pairs):
    total = None
    for i, j in pairs:
        term = jnp.dot(one[i], other[j], preferred_element_type=jnp.float32)
        total = term if total is None else total + term
    return total


FULL = ((2, 0), (0, 2), (1, 1), (1, 0), (0, 1), (0, 0))
SHORT = ((1, 0), (0, 1), (0, 0))


def y_kernel(count, places, spans, aliased):
    def kernel(*refs):
        number = len(places)
        blocks = dict(zip(places, refs))
        inner = [ref[...] for ref in refs[number : number + 3]]
        outer = [ref[...] for ref in refs[number + 3 : number + 6]]
        out, result, sems = refs[number + 6 + aliased :]
        fields, _, rows, columns = refs[0].shape
        total = count * columns
        me = lax.axis_index("gy")
        copies = []

        def piece(lane):
            block, at = divmod(lane % total, columns)
            return terms(blocks[block][:, 0, :, at : at + LANES].reshape(fields * rows, LANES))

        def send(first, last, base):
            block, at = divmod(first % total, columns)
            to = pl.multiple_of(lax.rem(me + block, count) * columns + at, LANES)
            copy = pltpu.make_async_copy(
                result.at[:, :, :, pl.ds(base, last - first)],
                out.at[:, :, :, pl.ds(to, last - first)],
                sems.at[len(copies)],
            )
            copy.start()
            copies.append(copy)

        base = 0
        for first, last in spans:
            sent = first
            tile = {lane: piece(lane) for lane in range(first - LANES, first + LANES, LANES)}
            for lane in range(first, last, UNIT):
                for step in (lane + LANES, lane + UNIT):
                    if step not in tile:
                        tile[step] = piece(step)
                middle = [jnp.concatenate([tile[lane][t], tile[lane + LANES][t]], axis=1) for t in range(3)]
                sides = [jnp.concatenate([tile[lane - LANES][t], tile[lane + UNIT][t]], axis=1) for t in range(2)]
                solved = product(sides, outer, SHORT) + product(middle, inner, FULL)
                at = base + lane - first
                result[:, 0, :, at : at + UNIT] = solved.reshape(fields, rows, UNIT)
                edge = min((sent // columns + 1) * columns, last)
                while edge <= lane + UNIT and sent < edge:
                    send(sent, edge, base + sent - first)
                    sent, edge = edge, min((edge // columns + 1) * columns, last)
            base += last - first
        for copy in copies:
            copy.wait()

    return kernel


def y_call(parts, count, places, spans, matrices, partial):
    operands = [*(parts[place] for place in places), *matrices]
    fields, slab, rows, columns = operands[0].shape
    width = sum(last - first for first, last in spans)
    pieces = sum(-(-last // columns) - first // columns for first, last in spans)
    vmem = pl.BlockSpec(memory_space=pltpu.VMEM)
    hbm = pl.BlockSpec(memory_space=pl.ANY)
    aliased = partial is not None
    size = fields * rows * width
    return pl.pallas_call(
        y_kernel(count, places, spans, int(aliased)),
        out_shape=jax.ShapeDtypeStruct((fields, slab, rows, count * columns), jnp.float32),
        in_specs=[vmem] * len(operands) + [hbm] * aliased,
        out_specs=hbm,
        scratch_shapes=[
            pltpu.VMEM((fields, slab, rows, width), jnp.float32),
            pltpu.SemaphoreType.DMA((pieces,)),
        ],
        input_output_aliases={len(operands): 0} if aliased else {},
        compiler_params=pltpu.CompilerParams(vmem_limit_bytes=LIMIT),
        cost_estimate=pl.CostEstimate(
            flops=9 * 2 * 256 * size, bytes_accessed=8 * size, transcendentals=0
        ),
    )(*[pltpu.with_memory_space_constraint(x, pltpu.VMEM) for x in operands], *([partial] if aliased else []))


def split_band():
    matrix = band()
    inner = matrix[LANES : LANES + UNIT]
    outer = np.concatenate([matrix[:LANES], matrix[LANES + UNIT :]], axis=0)
    pieces = []
    for values in (inner, outer):
        for _ in range(3):
            piece = values.astype(jnp.bfloat16)
            values = values - piece.astype(np.float32)
            pieces.append(jnp.asarray(piece))
    return pieces


def body(fields):
    count = lax.axis_size("gy")
    ring = lax.axis_size("gx")
    depth, slab, rows, columns = fields.shape
    part = rows // count
    value = {}
    matrices = split_band()
    source = pltpu.with_memory_space_constraint(fields, pltpu.HBM)
    cuts = {}
    for group in GROUPS:
        number = len(group)
        got = pl.pallas_call(
            cut_kernel(count, group, ((0, depth),)),
            out_shape=[pltpu.VMEM((depth, slab, part, columns), jnp.float32)] * number,
            in_specs=[pl.BlockSpec(memory_space=pl.ANY)],
            out_specs=[pl.BlockSpec(memory_space=pltpu.VMEM)] * number,
            scratch_shapes=[pltpu.SemaphoreType.DMA((number,))],
            compiler_params=pltpu.CompilerParams(vmem_limit_bytes=2**23),
            cost_estimate=pl.CostEstimate(flops=0, bytes_accessed=2 * 4 * number * depth * part * columns, transcendentals=0),
        )(source)
        cuts.update(zip(group, got))
        if group is not GROUPS[-1]:
            fields, cuts[group[-1]] = lax.optimization_barrier((fields, cuts[group[-1]]))
            source = pltpu.with_memory_space_constraint(fields, pltpu.HBM)
    value["y0"] = cuts[0]
    vmem = pl.BlockSpec(memory_space=pltpu.VMEM)
    c, e = columns, LANES
    plans = {
        3: {
            "A": ([3, 4, 5, 0], ((3 * c + e, 6 * c - e), (8 * c + e, 9 * c - e))),
            "B": ([2, 3, 5, 6], ((2 * c + e, 3 * c + e), (6 * c - e, 7 * c - e))),
            "C": ([6, 7, 0, 1, 2], ((7 * c - e, 8 * c + e), (9 * c - e, 10 * c + e))),
        },
        2: {
            "A": ([2, 3, 4, 5, 6, 0], ((2 * c + e, 7 * c - e), (8 * c + e, 9 * c - e))),
            "C": ([6, 7, 0, 1, 2], ((7 * c - e, 8 * c + e), (9 * c - e, 10 * c + e))),
        },
        4: {
            "A": ([3, 2, 1, 0, 7, 6, 5], ((5 * c + e, 12 * c - e),)),
            "C": ([3, 4, 5], ((4 * c - e, 5 * c + e),)),
        },
    }[3]
    last = None

    def tie(x, deps):
        for dep in deps:
            x, value[dep] = lax.optimization_barrier((x, value[dep]))
        return x

    for name, deps in STEPS:
        if name[0] == "y":
            hop = int(name[1:])
            cut = tie(cuts[hop], deps)
            value[name] = lax.ppermute(cut, "gy", [(i, (i + hop) % count) for i in range(count)])
        elif name == "b":
            halo = tie(fields[:, :, rows - HALO :], deps)
            value[name] = lax.ppermute(halo, "gx", [(i, (i + 1) % ring) for i in range(ring)])
        elif name == "a":
            halo = tie(fields[:, :, :HALO], deps)
            value[name] = lax.ppermute(halo, "gx", [((i + 1) % ring, i) for i in range(ring)])
        elif name == "X":
            value[name] = pl.pallas_call(
                x_kernel,
                out_shape=jax.ShapeDtypeStruct(fields.shape, fields.dtype),
                in_specs=[vmem] * 3,
                out_specs=vmem,
                cost_estimate=pl.CostEstimate(
                    flops=20 * fields.size, bytes_accessed=8 * fields.size, transcendentals=0
                ),
            )(fields, tie(value["b"], deps), value["a"])
        else:
            places, spans = plans[name]
            parts = {place: value["y%d" % ((count - place) % count)] for place in places}
            parts[places[0]] = tie(parts[places[0]], deps)
            last = y_call(parts, count, places, spans, matrices, last)
            value[name] = last
    return (value["X"], last)


def solution(mesh):
    placed = (P(None, "gz", "gx", "gy"),)
    return jax.shard_map(
        body,
        mesh=mesh,
        in_specs=placed,
        out_specs=(P(None, "gz", "gx", "gy"), P(None, "gz", ("gx", "gy"), None)),
        check_vma=False,
    )
```

time: 96.2 us -> 69.3 us (0.72)
  waiting for transfers between devices: 51.7 us -> 27.6 us
  starting transfers between devices: 15.4 us -> 21.3 us
  Pallas kernels: 23.7 us -> 18.3 us
  local copies, waits for them, and re-layouts: 4.52 us -> 1.13 us
    ppermute x9, waiting for transfers between devices: 51.7 us -> 27.6 us  [the longest x7 24 us: body(): lax.ppermute(cut, 'gy', [(i, (i + hop) % count) for i in range(count)])]
    ppermute x9, starting transfers between devices: 15.4 us -> 21.3 us  [the longest x7 18.5 us: body(): lax.ppermute(cut, 'gy', [(i, (i + hop) % count) for i in range(count)])]
    pallas_call x1 -> x6, Pallas kernels: 16.4 us -> 11.1 us  [the longest x3 5.91 us: y_call(): pl.pallas_call(y_kernel(count, places, spans, int(aliased)), out_shape=ja...]
    dynamic_slice x1 -> x0, local copies, waits for them, and re-layouts: 2.72 us -> none  [block(): lax.dynamic_slice_in_dim(fields, lax.rem(owner, count) * part, part, 2)]
  transfers between devices with their start and end apart: 9 -> 9, of which waited for: 5 -> 5; matrix products, arithmetic and copies ran while one was open for 1% -> 2% of each run, Pallas kernels for 8% -> 22%
where the time goes in v2:
time: 69.3 us; the launch traced here: 69.1 us
  waiting for transfers between devices  27.6 us (40%)
  starting transfers between devices  21.3 us (31%)
  Pallas kernels  18.3 us (26%)
  local copies, waits for them, and re-layouts  1.13 us (2%)
  between operations  0.74 us (1%)
    ppermute x7, waiting for transfers between devices, body(): lax.ppermute(cut, 'gy', [(i, (i + hop) % count) for i in range(count)])  24 us
    ppermute x7, starting transfers between devices, body(): lax.ppermute(cut, 'gy', [(i, (i + hop) % count) for i in range(count)])  18.5 us
    pallas_call x1, Pallas kernels, body(): pl.pallas_call(x_kernel, out_shape=jax.ShapeDtypeStruct(fields.shape, fie...  7.22 us
    pallas_call x3, Pallas kernels, y_call(): pl.pallas_call(y_kernel(count, places, spans, int(aliased)), out_shape=ja...  5.91 us
    pallas_call x3, Pallas kernels, body(): pl.pallas_call(cut_kernel(count, group, ((0, depth),)), out_shape=[pltpu....  5.19 us
    ppermute x1, starting transfers between devices, body(): lax.ppermute(halo, 'gx', [(i, (i + 1) % ring) for i in range(ring)])  2.77 us
    ppermute x1, waiting for transfers between devices, body(): lax.ppermute(halo, 'gx', [((i + 1) % ring, i) for i in range(ring)])  2.73 us
  transfers between devices with their start and end apart: 9, of which 5 were waited for; matrix products, arithmetic and copies ran while one was open for 2% of the time, Pallas kernels for 22%

profile of v2, /device:TPU:1, one launch (start us, length us, event | category | flops | bytes accessed | tf_op | source)
XLA Modules:
  0.0 69.1 jit_solution(17076071238492594308)
XLA Ops:
  0.6 1.0 %shard_map.86 = f32[5,1,32,512]{3,2,1,0:T(8,128)S(1)} custom-call(f32[5,1,256,512]{3,2,1,0:T(8,128)} %cells), custom_call_target="tpu_custom_call" | custom-call | bytes 655360 | tf_op jit(solution)/shard_map/pallas_call | solution.py:237
  1.6 7.8 %collective-permute-start.3 = (f32[5,1,32,512]{3,2,1,0:T(8,128)S(1)}, f32[5,1,32,512]{3,2,1,0:T(8,128)S(1)}, u32[]{:S(2)}, u32[]{:S(2)}) collective-permute-start(f32[5,1,32,512]{3,2,1,0:T(8,128)S(1)} %shard_map.86), channel_id=1, source_target_pairs={{0,8},{2,10},{4,12},{6,14},{8,0},{10,2},{12,4},{14,6},{1,9},{3,11}... | collective-permute-start | bytes 983048 | tf_op jit(solution)/shard_map/ppermute | solution.py:279
  9.5 1.9 %shard_map.87 = (f32[5,1,32,512]{3,2,1,0:T(8,128)}, f32[5,1,32,512]{3,2,1,0:T(8,128)}) custom-call(f32[5,1,256,512]{3,2,1,0:T(8,128)} %cells), custom_call_target="tpu_custom_call" | custom-call | bytes 1310720 | tf_op jit(solution)/shard_map/pallas_call | solution.py:237
  11.4 0.1 collective-permute-start.6
  11.5 3.3 %collective-permute-start = (f32[5,1,32,512]{3,2,1,0:T(8,128)}, f32[5,1,32,512]{3,2,1,0:T(8,128)S(1)}, u32[]{:S(2)}, u32[]{:S(2)}) collective-permute-start(f32[5,1,32,512]{3,2,1,0:T(8,128)} %get-tuple-element.29), channel_id=1, source_target_pairs={{0,6},{2,8},{4,10},{6,12},{8,14},{10,0},{12,2},{14,4},{1,7},{3,9},... | collective-permute-start | bytes 983048 | tf_op jit(solution)/shard_map/ppermute | solution.py:279
  14.7 1.1 %fusion = (f32[5,1,24,512]{3,2,1,0:T(8,128)S(1)}, f32[5,1,24,512]{3,2,1,0:T(8,128)S(1)}) fusion(f32[5,1,256,512]{3,2,1,0:T(8,128)} %cells), kind=kLoop, calls=%fused_computation | loop fusion | bytes 983040 | tf_op jit(solution)/shard_map/slice | solution.py:284
  15.8 2.8 %collective-permute-start.1 = (f32[5,1,24,512]{3,2,1,0:T(8,128)S(1)}, f32[5,1,24,512]{3,2,1,0:T(8,128)S(1)}, u32[]{:S(2)}, u32[]{:S(2)}) collective-permute-start(f32[5,1,24,512]{3,2,1,0:T(8,128)S(1)} %get-tuple-element.49), channel_id=1, source_target_pairs={{0,16},{16,32},{32,48},{48,64},{64,80},{80,96},{96,112},{112,128},... | collective-permute-start | bytes 737288 | tf_op jit(solution)/shard_map/ppermute | solution.py:282
  18.6 0.0 collective-permute-start.2
  18.6 2.3 %shard_map.88 = (f32[5,1,32,512]{3,2,1,0:T(8,128)}, f32[5,1,32,512]{3,2,1,0:T(8,128)}, f32[5,1,32,512]{3,2,1,0:T(8,128)S(1)}, f32[5,1,32,512]{3,2,1,0:T(8,128)S(1)}, f32[5,1,32,512]{3,2,1,0:T(8,128)S(1)}) custom-call(f32[5,1,256,512]{3,2,1,0:T(8,128)} %cells), custom_call_target="tpu_custom_call" | custom-call | bytes 3276800 | tf_op jit(solution)/shard_map/pallas_call | solution.py:237
  20.9 0.0 collective-permute-done.3.refs_1_
  20.9 0.9 %collective-permute-done.1.below = f32[5,1,24,512]{3,2,1,0:T(8,128)S(1)} collective-permute-done((f32[5,1,24,512]{3,2,1,0:T(8,128)S(1)}, f32[5,1,24,512]{3,2,1,0:T(8,128)S(1)}, u32[]{:S(2)}, u32[]{:S(2)}) %collective-permute-start.1) | collective-permute-done | bytes 245792 | tf_op jit(solution)/shard_map/ppermute | solution.py:282
  21.8 0.0 copy-start.4
  21.8 0.0 copy-start.5
  21.8 2.7 %collective-permute-done.2.above = f32[5,1,24,512]{3,2,1,0:T(8,128)S(1)} collective-permute-done((f32[5,1,24,512]{3,2,1,0:T(8,128)S(1)}, f32[5,1,24,512]{3,2,1,0:T(8,128)S(1)}, u32[]{:S(2)}, u32[]{:S(2)}) %collective-permute-start.2) | collective-permute-done | bytes 245792 | tf_op jit(solution)/shard_map/ppermute | solution.py:285
  24.5 0.0 copy-done.6
  24.5 4.3 %collective-permute-start.8 = (f32[5,1,32,512]{3,2,1,0:T(8,128)}, f32[5,1,32,512]{3,2,1,0:T(8,128)S(1)}, u32[]{:S(2)}, u32[]{:S(2)}) collective-permute-start(f32[5,1,32,512]{3,2,1,0:T(8,128)} %get-tuple-element.44), channel_id=1, source_target_pairs={{0,12},{2,14},{4,0},{6,2},{8,4},{10,6},{12,8},{14,10},{1,13},{3,15... | collective-permute-start | bytes 983048 | tf_op jit(solution)/shard_map/ppermute | solution.py:279
  28.9 0.0 copy-done.7
  28.9 1.6 %collective-permute-start.4 = (f32[5,1,32,512]{3,2,1,0:T(8,128)}, f32[5,1,32,512]{3,2,1,0:T(8,128)S(1)}, u32[]{:S(2)}, u32[]{:S(2)}) collective-permute-start(f32[5,1,32,512]{3,2,1,0:T(8,128)} %get-tuple-element.35), channel_id=1, source_target_pairs={{0,4},{2,6},{4,8},{6,10},{8,12},{10,14},{12,0},{14,2},{1,5},{3,7},... | collective-permute-start | bytes 983048 | tf_op jit(solution)/shard_map/ppermute | solution.py:279
  30.4 7.2 %shard_map.89 = f32[5,1,256,512]{3,2,1,0:T(8,128)} custom-call(f32[5,1,256,512]{3,2,1,0:T(8,128)} %cells, f32[5,1,24,512]{3,2,1,0:T(8,128)} %copy-done.6, f32[5,1,24,512]{3,2,1,0:T(8,128)} %copy-done.7), custom_call_target="tpu_custom_call" | custom-call | flops 13107200 | bytes 5242880 | tf_op jit(solution)/shard_map/pallas_call | solution.py:287
  37.7 13.1 %collective-permute-done.refs_2_ = f32[5,1,32,512]{3,2,1,0:T(8,128)S(1)} collective-permute-done((f32[5,1,32,512]{3,2,1,0:T(8,128)}, f32[5,1,32,512]{3,2,1,0:T(8,128)S(1)}, u32[]{:S(2)}, u32[]{:S(2)}) %collective-permute-start) | collective-permute-done | bytes 327712 | tf_op jit(solution)/shard_map/ppermute | solution.py:279
  50.7 0.0 collective-permute-done.6.refs_0_.refs_1_
  50.7 0.0 collective-permute-start.7
  50.7 1.5 %collective-permute-start.5 = (f32[5,1,32,512]{3,2,1,0:T(8,128)S(1)}, f32[5,1,32,512]{3,2,1,0:T(8,128)S(1)}, u32[]{:S(2)}, u32[]{:S(2)}) collective-permute-start(f32[5,1,32,512]{3,2,1,0:T(8,128)S(1)} %get-tuple-element.36), channel_id=1, source_target_pairs={{0,2},{2,4},{4,6},{6,8},{8,10},{10,12},{12,14},{14,0},{1,3},{3,5},... | collective-permute-start | bytes 983048 | tf_op jit(solution)/shard_map/ppermute | solution.py:279
  52.2 0.0 copy-done
  52.2 0.0 copy-done.2
  52.2 2.1 %shard_map.90.refs_10_ = f32[5,1,32,4096]{3,2,1,0:T(8,128)} custom-call(f32[5,1,32,512]{3,2,1,0:T(8,128)S(1)} %collective-permute-done.6.refs_0_.refs_1_, f32[5,1,32,512]{3,2,1,0:T(8,128)S(1)} %collective-permute-done.3.refs_1_, f32[5,1,32,512]{3,2,1,0:T(8,128)S(1)} %collective-permute-done.refs_2_, f32[5,1,32,512]{3,2,1,0:T(8,128)S(1)} %get-tuple-element.37.refs_3_.refs_2_, ...), custom_call_target="tpu_custom_call" | custom-call | flops 1132462080 | bytes 1966080 | tf_op jit(solution)/shard_map/pallas_call | solution.py:196
  54.3 5.9 %collective-permute-done.8.refs_0_.refs_4_ = f32[5,1,32,512]{3,2,1,0:T(8,128)S(1)} collective-permute-done((f32[5,1,32,512]{3,2,1,0:T(8,128)}, f32[5,1,32,512]{3,2,1,0:T(8,128)S(1)}, u32[]{:S(2)}, u32[]{:S(2)}) %collective-permute-start.8) | collective-permute-done | bytes 327712 | tf_op jit(solution)/shard_map/ppermute | solution.py:279
  60.2 0.0 collective-permute-done.4.refs_3_.refs_0_
  60.2 1.7 %shard_map.91.refs_11_ = f32[5,1,32,4096]{3,2,1,0:T(8,128)} custom-call(f32[5,1,32,512]{3,2,1,0:T(8,128)S(1)} %collective-permute-done.8.refs_0_.refs_4_, f32[5,1,32,512]{3,2,1,0:T(8,128)S(1)} %collective-permute-done.6.refs_0_.refs_1_, f32[5,1,32,512]{3,2,1,0:T(8,128)S(1)} %collective-permute-done.refs_2_, ...), custom_call_target="tpu_custom_call", output_to_operand_aliasing={{}: (10, {})} | custom-call | flops 754974720 | bytes 1310720 | tf_op jit(solution)/shard_map/pallas_call | solution.py:196
  61.9 5.0 %collective-permute-done.7.refs_3_ = f32[5,1,32,512]{3,2,1,0:T(8,128)S(1)} collective-permute-done((f32[5,1,32,512]{3,2,1,0:T(8,128)S(1)}, f32[5,1,32,512]{3,2,1,0:T(8,128)S(1)}, u32[]{:S(2)}, u32[]{:S(2)}) %collective-permute-start.7) | collective-permute-done | bytes 327712 | tf_op jit(solution)/shard_map/ppermute | solution.py:279
  67.0 0.0 collective-permute-done.5.refs_1_
  67.0 2.1 %shard_map.92 = f32[5,1,32,4096]{3,2,1,0:T(8,128)} custom-call(f32[5,1,32,512]{3,2,1,0:T(8,128)S(1)} %collective-permute-done.4.refs_3_.refs_0_, f32[5,1,32,512]{3,2,1,0:T(8,128)S(1)} %collective-permute-done.5.refs_1_, f32[5,1,32,512]{3,2,1,0:T(8,128)S(1)} %get-tuple-element.37.refs_3_.refs_2_, ...), custom_call_target="tpu_custom_call", output_to_operand_aliasing={{}: (11, {})} | custom-call | flops 1132462080 | bytes 1966080 | tf_op jit(solution)/shard_map/pallas_call | solution.py:196
  (10 shorter events, 0.0 us)
Async XLA Ops:
  1.6 19.3 %collective-permute-start.3 = (f32[5,1,32,512]{3,2,1,0:T(8,128)S(1)}, f32[5,1,32,512]{3,2,1,0:T(8,128)S(1)}, u32[]{:S(2)}, u32[]{:S(2)}) collective-permute-start(f32[5,1,32,512]{3,2,1,0:T(8,128)S(1)} %shard_map.86), channel_id=1, source_target_pairs={{0,8},{2,10},{4,12},{6,14},{8,0},{10,2},{12,4},{14,6},{1,9},{3,11}... | collective-permute-start | bytes 983048 | tf_op jit(solution)/shard_map/ppermute | solution.py:279
  11.4 39.3 %collective-permute-start.6 = (f32[5,1,32,512]{3,2,1,0:T(8,128)}, f32[5,1,32,512]{3,2,1,0:T(8,128)S(1)}, u32[]{:S(2)}, u32[]{:S(2)}) collective-permute-start(f32[5,1,32,512]{3,2,1,0:T(8,128)} %get-tuple-element.39), channel_id=1, source_target_pairs={{0,10},{2,12},{4,14},{6,0},{8,2},{10,4},{12,6},{14,8},{1,11},{3,13... | collective-permute-start | bytes 983048 | tf_op jit(solution)/shard_map/ppermute | solution.py:279
  11.5 39.2 %collective-permute-start = (f32[5,1,32,512]{3,2,1,0:T(8,128)}, f32[5,1,32,512]{3,2,1,0:T(8,128)S(1)}, u32[]{:S(2)}, u32[]{:S(2)}) collective-permute-start(f32[5,1,32,512]{3,2,1,0:T(8,128)} %get-tuple-element.29), channel_id=1, source_target_pairs={{0,6},{2,8},{4,10},{6,12},{8,14},{10,0},{12,2},{14,4},{1,7},{3,9},... | collective-permute-start | bytes 983048 | tf_op jit(solution)/shard_map/ppermute | solution.py:279
  15.8 5.9 %collective-permute-start.1 = (f32[5,1,24,512]{3,2,1,0:T(8,128)S(1)}, f32[5,1,24,512]{3,2,1,0:T(8,128)S(1)}, u32[]{:S(2)}, u32[]{:S(2)}) collective-permute-start(f32[5,1,24,512]{3,2,1,0:T(8,128)S(1)} %get-tuple-element.49), channel_id=1, source_target_pairs={{0,16},{16,32},{32,48},{48,64},{64,80},{80,96},{96,112},{112,128},... | collective-permute-start | bytes 737288 | tf_op jit(solution)/shard_map/ppermute | solution.py:282
  18.6 5.9 %collective-permute-start.2 = (f32[5,1,24,512]{3,2,1,0:T(8,128)S(1)}, f32[5,1,24,512]{3,2,1,0:T(8,128)S(1)}, u32[]{:S(2)}, u32[]{:S(2)}) collective-permute-start(f32[5,1,24,512]{3,2,1,0:T(8,128)S(1)} %get-tuple-element.48), channel_id=1, source_target_pairs={{16,0},{32,16},{48,32},{64,48},{80,64},{96,80},{112,96},{128,112},... | collective-permute-start | bytes 737288 | tf_op jit(solution)/shard_map/ppermute | solution.py:285
  21.8 2.8 %copy-start.6 = (f32[5,1,24,512]{3,2,1,0:T(8,128)}, f32[5,1,24,512]{3,2,1,0:T(8,128)S(1)}, u32[]{:S(2)}) copy-start(f32[5,1,24,512]{3,2,1,0:T(8,128)S(1)} %collective-permute-done.1.below) | copy-start | bytes 737284
  21.8 30.4 %copy-start = (bf16[256,256]{1,0:T(8,128)(2,1)S(1)}, bf16[256,256]{1,0:T(8,128)(2,1)}, u32[]{:S(2)}) copy-start(bf16[256,256]{1,0:T(8,128)(2,1)} %constant.17.clone.refs_9_.refs_10_) | copy-start | bytes 393220
  21.8 30.4 %copy-start.1 = (bf16[256,256]{1,0:T(8,128)(2,1)S(1)}, bf16[256,256]{1,0:T(8,128)(2,1)}, u32[]{:S(2)}) copy-start(bf16[256,256]{1,0:T(8,128)(2,1)} %constant.16.clone.refs_8_.refs_9_) | copy-start | bytes 393220
  21.8 30.4 %copy-start.2 = (bf16[256,256]{1,0:T(8,128)(2,1)S(1)}, bf16[256,256]{1,0:T(8,128)(2,1)}, u32[]{:S(2)}) copy-start(bf16[256,256]{1,0:T(8,128)(2,1)} %constant.15.clone.refs_7_.refs_8_) | copy-start | bytes 393220
  21.8 30.4 %copy-start.3 = (bf16[256,256]{1,0:T(8,128)(2,1)S(1)}, bf16[256,256]{1,0:T(8,128)(2,1)}, u32[]{:S(2)}) copy-start(bf16[256,256]{1,0:T(8,128)(2,1)} %constant.14.clone.refs_6_.refs_7_) | copy-start | bytes 393220
  21.8 30.4 %copy-start.4 = (bf16[256,256]{1,0:T(8,128)(2,1)S(1)}, bf16[256,256]{1,0:T(8,128)(2,1)}, u32[]{:S(2)}) copy-start(bf16[256,256]{1,0:T(8,128)(2,1)} %constant.13.clone.refs_5_.refs_6_) | copy-start | bytes 393220
  21.8 30.4 %copy-start.5 = (bf16[256,256]{1,0:T(8,128)(2,1)S(1)}, bf16[256,256]{1,0:T(8,128)(2,1)}, u32[]{:S(2)}) copy-start(bf16[256,256]{1,0:T(8,128)(2,1)} %constant.12.clone.refs_4_.refs_5_) | copy-start | bytes 393220
  24.5 4.3 %copy-start.7 = (f32[5,1,24,512]{3,2,1,0:T(8,128)}, f32[5,1,24,512]{3,2,1,0:T(8,128)S(1)}, u32[]{:S(2)}) copy-start(f32[5,1,24,512]{3,2,1,0:T(8,128)S(1)} %collective-permute-done.2.above) | copy-start | bytes 737284
  24.5 35.7 %collective-permute-start.8 = (f32[5,1,32,512]{3,2,1,0:T(8,128)}, f32[5,1,32,512]{3,2,1,0:T(8,128)S(1)}, u32[]{:S(2)}, u32[]{:S(2)}) collective-permute-start(f32[5,1,32,512]{3,2,1,0:T(8,128)} %get-tuple-element.44), channel_id=1, source_target_pairs={{0,12},{2,14},{4,0},{6,2},{8,4},{10,6},{12,8},{14,10},{1,13},{3,15... | collective-permute-start | bytes 983048 | tf_op jit(solution)/shard_map/ppermute | solution.py:279
  28.9 31.4 %collective-permute-start.4 = (f32[5,1,32,512]{3,2,1,0:T(8,128)}, f32[5,1,32,512]{3,2,1,0:T(8,128)S(1)}, u32[]{:S(2)}, u32[]{:S(2)}) collective-permute-start(f32[5,1,32,512]{3,2,1,0:T(8,128)} %get-tuple-element.35), channel_id=1, source_target_pairs={{0,4},{2,6},{4,8},{6,10},{8,12},{10,14},{12,0},{14,2},{1,5},{3,7},... | collective-permute-start | bytes 983048 | tf_op jit(solution)/shard_map/ppermute | solution.py:279
  50.7 16.2 %collective-permute-start.7 = (f32[5,1,32,512]{3,2,1,0:T(8,128)S(1)}, f32[5,1,32,512]{3,2,1,0:T(8,128)S(1)}, u32[]{:S(2)}, u32[]{:S(2)}) collective-permute-start(f32[5,1,32,512]{3,2,1,0:T(8,128)S(1)} %get-tuple-element.40), channel_id=1, source_target_pairs={{0,14},{2,0},{4,2},{6,4},{8,6},{10,8},{12,10},{14,12},{1,15},{3,1}... | collective-permute-start | bytes 983048 | tf_op jit(solution)/shard_map/ppermute | solution.py:279
  50.7 16.2 %collective-permute-start.5 = (f32[5,1,32,512]{3,2,1,0:T(8,128)S(1)}, f32[5,1,32,512]{3,2,1,0:T(8,128)S(1)}, u32[]{:S(2)}, u32[]{:S(2)}) collective-permute-start(f32[5,1,32,512]{3,2,1,0:T(8,128)S(1)} %get-tuple-element.36), channel_id=1, source_target_pairs={{0,2},{2,4},{4,6},{6,8},{8,10},{10,12},{12,14},{14,0},{1,3},{3,5},... | collective-permute-start | bytes 983048 | tf_op jit(solution)/shard_map/ppermute | solution.py:279

commit v3 on v2

--- a/solution.py
+++ b/solution.py
@@ -8,7 +8,8 @@
 
 LEVELS = 4
 HALO = 24
-LIMIT = 16 * 2**20
+LIMIT = 8 * 2**20
+STACK = 400
 STEPS = (
     ("y4", ()),
     ("b", ()),
@@ -18,13 +19,18 @@
     ("y5", ()),
     ("y2", ("y4", "b", )),
     ("y6", ("y4", "a", )),
-    ("y1", ("y3", "X", )),
-    ("y7", ("y5", )),
+    ("y1p", ("y3", "X", )),
+    ("y7p", ("y5", )),
+    ("y1q", ("y3", )),
+    ("y7q", ("y6", )),
     ("A", ()),
     ("B", ()),
     ("C", ()),
+    ("D", ()),
 )
-GROUPS = ((4,), (3, 5), (2, 6, 1, 7, 0))
+GROUPS = ((4,), (3, 5), (2, 6, "1p", "7p", "1q", "7q", 0))
+SPLIT = 3
+XLIMIT = 12 * 2**20
 LANES = 128
 UNIT = 256
 REACH = 17
@@ -93,20 +99,17 @@
     lax.fori_loop(0, fields * tiles, step, 0)
 
 
-def cut_kernel(count, hops, chunks):
+def cut_kernel(count, pieces):
     def kernel(fields, *refs):
         outs, sems = refs[:-1], refs[-1]
         me = lax.axis_index("gy")
         copies = []
-        for first, last in chunks:
-            for hop in hops:
-                rows = outs[len(copies)].shape[2]
-                at = pl.multiple_of(lax.rem(me + hop, count) * rows, rows)
-                copy = pltpu.make_async_copy(
-                    fields.at[first:last, :, pl.ds(at, rows), :], outs[len(copies)], sems.at[len(copies)]
-                )
-                copy.start()
-                copies.append(copy)
+        for number, (hop, first, last) in enumerate(pieces):
+            rows = outs[number].shape[2]
+            at = pl.multiple_of(lax.rem(me + hop, count) * rows, rows)
+            copy = pltpu.make_async_copy(fields.at[first:last, :, pl.ds(at, rows), :], outs[number], sems.at[number])
+            copy.start()
+            copies.append(copy)
         for copy in copies:
             copy.wait()
 
@@ -133,60 +136,72 @@
 SHORT = ((1, 0), (0, 1), (0, 0))
 
 
-def y_kernel(count, places, spans, aliased):
+def y_kernel(count, places, starts, first_field, fields, spans, aliased):
     def kernel(*refs):
         number = len(places)
         blocks = dict(zip(places, refs))
+        begin = dict(zip(places, starts))
         inner = [ref[...] for ref in refs[number : number + 3]]
         outer = [ref[...] for ref in refs[number + 3 : number + 6]]
         out, result, sems = refs[number + 6 + aliased :]
-        fields, _, rows, columns = refs[0].shape
+        _, _, rows, columns = refs[0].shape
         total = count * columns
         me = lax.axis_index("gy")
         copies = []
 
         def piece(lane):
             block, at = divmod(lane % total, columns)
-            return terms(blocks[block][:, 0, :, at : at + LANES].reshape(fields * rows, LANES))
+            low = first_field - begin[block]
+            return terms(blocks[block][low : low + fields, 0, :, at : at + LANES].reshape(fields * rows, LANES))
 
         def send(first, last, base):
             block, at = divmod(first % total, columns)
             to = pl.multiple_of(lax.rem(me + block, count) * columns + at, LANES)
             copy = pltpu.make_async_copy(
                 result.at[:, :, :, pl.ds(base, last - first)],
-                out.at[:, :, :, pl.ds(to, last - first)],
+                out.at[pl.ds(first_field, fields), :, :, pl.ds(to, last - first)],
                 sems.at[len(copies)],
             )
             copy.start()
             copies.append(copy)
 
-        base = 0
+        size = fields * rows
+        units, base = [], 0
         for first, last in spans:
-            sent = first
-            tile = {lane: piece(lane) for lane in range(first - LANES, first + LANES, LANES)}
-            for lane in range(first, last, UNIT):
-                for step in (lane + LANES, lane + UNIT):
-                    if step not in tile:
-                        tile[step] = piece(step)
-                middle = [jnp.concatenate([tile[lane][t], tile[lane + LANES][t]], axis=1) for t in range(3)]
-                sides = [jnp.concatenate([tile[lane - LANES][t], tile[lane + UNIT][t]], axis=1) for t in range(2)]
-                solved = product(sides, outer, SHORT) + product(middle, inner, FULL)
-                at = base + lane - first
-                result[:, 0, :, at : at + UNIT] = solved.reshape(fields, rows, UNIT)
-                edge = min((sent // columns + 1) * columns, last)
-                while edge <= lane + UNIT and sent < edge:
-                    send(sent, edge, base + sent - first)
-                    sent, edge = edge, min((edge // columns + 1) * columns, last)
+            tile = {lane: piece(lane) for lane in range(first - LANES, last + LANES, LANES)}
+            units += [(lane, base + lane - first, first, last, tile) for lane in range(first, last, UNIT)]
             base += last - first
+
+        def stacked(shifts, term, group):
+            return jnp.concatenate(
+                [jnp.concatenate([tile[lane + s][term] for s in shifts], axis=1) for lane, _, _, _, tile in group], axis=0
+            )
+
+        together = max(1, STACK // size)
+        sent = {first: first for first, _ in spans}
+        for start in range(0, len(units), together):
+            group = units[start : start + together]
+            middle = [stacked((0, LANES), t, group) for t in range(3)]
+            sides = [stacked((-LANES, UNIT), t, group) for t in range(2)]
+            solved = product(sides, outer, SHORT) + product(middle, inner, FULL)
+            for number, (lane, at, first, last, _) in enumerate(group):
+                part = solved[number * size : (number + 1) * size]
+                result[:, 0, :, at : at + UNIT] = part.reshape(fields, rows, UNIT)
+                while sent[first] < last:
+                    edge = min((sent[first] // columns + 1) * columns, last)
+                    if edge > lane + UNIT:
+                        break
+                    send(sent[first], edge, at - lane + sent[first])
+                    sent[first] = edge
         for copy in copies:
             copy.wait()
 
     return kernel
 
 
-def y_call(parts, count, places, spans, matrices, partial):
+def y_call(parts, count, places, starts, first_field, fields, depth, spans, matrices, partial):
     operands = [*(parts[place] for place in places), *matrices]
-    fields, slab, rows, columns = operands[0].shape
+    _, slab, rows, columns = operands[0].shape
     width = sum(last - first for first, last in spans)
     pieces = sum(-(-last // columns) - first // columns for first, last in spans)
     vmem = pl.BlockSpec(memory_space=pltpu.VMEM)
@@ -194,8 +209,8 @@
     aliased = partial is not None
     size = fields * rows * width
     return pl.pallas_call(
-        y_kernel(count, places, spans, int(aliased)),
-        out_shape=jax.ShapeDtypeStruct((fields, slab, rows, count * columns), jnp.float32),
+        y_kernel(count, places, starts, first_field, fields, spans, int(aliased)),
+        out_shape=jax.ShapeDtypeStruct((depth, slab, rows, count * columns), jnp.float32),
         in_specs=[vmem] * len(operands) + [hbm] * aliased,
         out_specs=hbm,
         scratch_shapes=[
@@ -232,39 +247,43 @@
     matrices = split_band()
     source = pltpu.with_memory_space_constraint(fields, pltpu.HBM)
     cuts = {}
+    def piece_of(hop):
+        name = "y%s" % hop
+        if name[-1] == "p":
+            return (int(hop[:-1]), 0, SPLIT)
+        if name[-1] == "q":
+            return (int(hop[:-1]), SPLIT, depth)
+        return (int(hop), 0, depth)
+
     for group in GROUPS:
-        number = len(group)
+        pieces = [piece_of(str(hop)) for hop in group]
         got = pl.pallas_call(
-            cut_kernel(count, group, ((0, depth),)),
-            out_shape=[pltpu.VMEM((depth, slab, part, columns), jnp.float32)] * number,
+            cut_kernel(count, pieces),
+            out_shape=[
+                jax.ShapeDtypeStruct((last - first, slab, part, columns), jnp.float32) for _, first, last in pieces
+            ],
             in_specs=[pl.BlockSpec(memory_space=pl.ANY)],
-            out_specs=[pl.BlockSpec(memory_space=pltpu.VMEM)] * number,
-            scratch_shapes=[pltpu.SemaphoreType.DMA((number,))],
-            compiler_params=pltpu.CompilerParams(vmem_limit_bytes=2**23),
-            cost_estimate=pl.CostEstimate(flops=0, bytes_accessed=2 * 4 * number * depth * part * columns, transcendentals=0),
+            out_specs=[pl.BlockSpec(memory_space=pl.ANY)] * len(pieces),
+            scratch_shapes=[pltpu.SemaphoreType.DMA((len(pieces),))],
+            compiler_params=pltpu.CompilerParams(vmem_limit_bytes=2**20),
+            cost_estimate=pl.CostEstimate(flops=0, bytes_accessed=2 * 4 * len(pieces) * depth * part * columns, transcendentals=0),
         )(source)
-        cuts.update(zip(group, got))
+        cuts.update(zip((str(hop) for hop in group), got))
         if group is not GROUPS[-1]:
-            fields, cuts[group[-1]] = lax.optimization_barrier((fields, cuts[group[-1]]))
+            fields, cuts[str(group[-1])] = lax.optimization_barrier((fields, cuts[str(group[-1])]))
             source = pltpu.with_memory_space_constraint(fields, pltpu.HBM)
-    value["y0"] = cuts[0]
+    value["y0"] = cuts["0"]
     vmem = pl.BlockSpec(memory_space=pltpu.VMEM)
     c, e = columns, LANES
+    inner = ((3 * c + e, 6 * c - e), (8 * c + e, 9 * c - e))
+    ring_2 = ((2 * c + e, 3 * c + e), (6 * c - e, 7 * c - e))
+    ring_1 = ((7 * c - e, 8 * c + e), (9 * c - e, 10 * c + e))
     plans = {
-        3: {
-            "A": ([3, 4, 5, 0], ((3 * c + e, 6 * c - e), (8 * c + e, 9 * c - e))),
-            "B": ([2, 3, 5, 6], ((2 * c + e, 3 * c + e), (6 * c - e, 7 * c - e))),
-            "C": ([6, 7, 0, 1, 2], ((7 * c - e, 8 * c + e), (9 * c - e, 10 * c + e))),
-        },
-        2: {
-            "A": ([2, 3, 4, 5, 6, 0], ((2 * c + e, 7 * c - e), (8 * c + e, 9 * c - e))),
-            "C": ([6, 7, 0, 1, 2], ((7 * c - e, 8 * c + e), (9 * c - e, 10 * c + e))),
-        },
-        4: {
-            "A": ([3, 2, 1, 0, 7, 6, 5], ((5 * c + e, 12 * c - e),)),
-            "C": ([3, 4, 5], ((4 * c - e, 5 * c + e),)),
-        },
-    }[3]
+        "A": ([3, 4, 5, 0], inner, ""),
+        "B": ([2, 3, 5, 6], ring_2, ""),
+        "C": ([6, 7, 0, 1, 2], ring_1, "p" if SPLIT else ""),
+        "D": ([6, 7, 0, 1, 2], ring_1, "q"),
+    }
     last = None
 
     def tie(x, deps):
@@ -274,8 +293,8 @@
 
     for name, deps in STEPS:
         if name[0] == "y":
-            hop = int(name[1:])
-            cut = tie(cuts[hop], deps)
+            hop = piece_of(name[1:])[0]
+            cut = tie(cuts[name[1:]], deps)
             value[name] = lax.ppermute(cut, "gy", [(i, (i + hop) % count) for i in range(count)])
         elif name == "b":
             halo = tie(fields[:, :, rows - HALO :], deps)
@@ -289,15 +308,25 @@
                 out_shape=jax.ShapeDtypeStruct(fields.shape, fields.dtype),
                 in_specs=[vmem] * 3,
                 out_specs=vmem,
+                compiler_params=pltpu.CompilerParams(vmem_limit_bytes=XLIMIT),
                 cost_estimate=pl.CostEstimate(
                     flops=20 * fields.size, bytes_accessed=8 * fields.size, transcendentals=0
                 ),
             )(fields, tie(value["b"], deps), value["a"])
         else:
-            places, spans = plans[name]
-            parts = {place: value["y%d" % ((count - place) % count)] for place in places}
+            places, spans, suffix = plans[name]
+            low, high = {"": (0, depth), "p": (0, SPLIT), "q": (SPLIT, depth)}[suffix]
+            parts, starts = {}, []
+            for place in places:
+                source_name = "y%d" % ((count - place) % count)
+                if source_name in value:
+                    starts.append(0)
+                else:
+                    source_name += suffix
+                    starts.append(low)
+                parts[place] = value[source_name]
             parts[places[0]] = tie(parts[places[0]], deps)
-            last = y_call(parts, count, places, spans, matrices, last)
+            last = y_call(parts, count, places, starts, low, high - low, depth, spans, matrices, last)
             value[name] = last
     return (value["X"], last)
 

time: 69.3 us -> 68.3 us (0.986)
  starting transfers between devices: 21.3 us -> 25.7 us
  waiting for transfers between devices: 27.6 us -> 24.7 us
  Pallas kernels: 18.3 us -> 15.9 us
    ppermute x7 -> x9, starting transfers between devices: 18.5 us -> 23.3 us  [body(): lax.ppermute(cut, 'gy', [(i, (i + hop) % count) for i in range(count)])]
    ppermute x1, waiting for transfers between devices: 2.73 us -> 0.01 us  [body(): lax.ppermute(halo, 'gx', [((i + 1) % ring, i) for i in range(ring)])]
    pallas_call x1, Pallas kernels: 7.22 us -> 5.33 us  [body(): pl.pallas_call(x_kernel, out_shape=jax.ShapeDtypeStruct(fields.shape, fie...]
    ppermute x1, starting transfers between devices: 2.77 us -> 1.27 us  [body(): lax.ppermute(halo, 'gx', [(i, (i + 1) % ring) for i in range(ring)])]
    ppermute x1, starting transfers between devices: 0.01 us -> 1.03 us  [body(): lax.ppermute(halo, 'gx', [((i + 1) % ring, i) for i in range(ring)])]
    ppermute x1, waiting for transfers between devices: 0.86 us -> 0.01 us  [body(): lax.ppermute(halo, 'gx', [(i, (i + 1) % ring) for i in range(ring)])]
    ppermute x7 -> x9, waiting for transfers between devices: 24 us -> 24.6 us  [body(): lax.ppermute(cut, 'gy', [(i, (i + hop) % count) for i in range(count)])]
    pallas_call x6 -> x7, Pallas kernels: 11.1 us -> 10.6 us  [the longest x4 7.05 us: y_call(): pl.pallas_call(y_kernel(count, places, starts, first_field, fields, spans...]
  transfers between devices with their start and end apart: 9 -> 11, of which waited for: 5 -> 4; matrix products, arithmetic and copies ran while one was open for 2% -> 2% of each run, Pallas kernels for 22% -> 20%
where the time goes in v3:
time: 68.3 us; the launch traced here: 68.1 us
  starting transfers between devices  25.7 us (38%)
  waiting for transfers between devices  24.7 us (36%)
  Pallas kernels  15.9 us (23%)
  local copies, waits for them, and re-layouts  1.15 us (2%)
  between operations  0.79 us (1%)
    ppermute x9, waiting for transfers between devices, body(): lax.ppermute(cut, 'gy', [(i, (i + hop) % count) for i in range(count)])  24.6 us
    ppermute x9, starting transfers between devices, body(): lax.ppermute(cut, 'gy', [(i, (i + hop) % count) for i in range(count)])  23.3 us
    pallas_call x4, Pallas kernels, y_call(): pl.pallas_call(y_kernel(count, places, starts, first_field, fields, spans...  7.05 us
    pallas_call x1, Pallas kernels, body(): pl.pallas_call(x_kernel, out_shape=jax.ShapeDtypeStruct(fields.shape, fie...  5.33 us
    pallas_call x3, Pallas kernels, body(): pl.pallas_call(cut_kernel(count, pieces), out_shape=[jax.ShapeDtypeStruct...  3.51 us
  transfers between devices with their start and end apart: 11, of which 4 were waited for; matrix products, arithmetic and copies ran while one was open for 2% of the time, Pallas kernels for 20%

profile of v3, /device:TPU:1, one launch (start us, length us, event | category | flops | bytes accessed | tf_op | source)
XLA Modules:
  0.0 68.1 jit_solution(9215981540333189921)
XLA Ops:
  0.6 1.0 %shard_map.86 = f32[5,1,32,512]{3,2,1,0:T(8,128)S(1)} custom-call(f32[5,1,256,512]{3,2,1,0:T(8,128)} %cells), custom_call_target="tpu_custom_call" | custom-call | bytes 655360 | tf_op jit(solution)/shard_map/pallas_call | solution.py:260
  1.6 0.0 copy-start
  1.6 7.8 %collective-permute-start.3 = (f32[5,1,32,512]{3,2,1,0:T(8,128)S(1)}, f32[5,1,32,512]{3,2,1,0:T(8,128)S(1)}, u32[]{:S(2)}, u32[]{:S(2)}) collective-permute-start(f32[5,1,32,512]{3,2,1,0:T(8,128)S(1)} %shard_map.86), channel_id=1, source_target_pairs={{0,8},{2,10},{4,12},{6,14},{8,0},{10,2},{12,4},{14,6},{1,9},{3,11}... | collective-permute-start | bytes 983048 | tf_op jit(solution)/shard_map/ppermute | solution.py:298
  9.5 1.1 %shard_map.87 = (f32[5,1,32,512]{3,2,1,0:T(8,128)S(1)}, f32[5,1,32,512]{3,2,1,0:T(8,128)S(1)}) custom-call(f32[5,1,256,512]{3,2,1,0:T(8,128)} %cells), custom_call_target="tpu_custom_call" | custom-call | bytes 1310720 | tf_op jit(solution)/shard_map/pallas_call | solution.py:260
  10.6 1.1 %fusion = (f32[5,1,24,512]{3,2,1,0:T(8,128)S(1)}, f32[5,1,24,512]{3,2,1,0:T(8,128)S(1)}) fusion(f32[5,1,256,512]{3,2,1,0:T(8,128)} %cells), kind=kLoop, calls=%fused_computation | loop fusion | bytes 983040 | tf_op jit(solution)/shard_map/slice | solution.py:303
  11.7 1.0 %collective-permute-start.2 = (f32[5,1,24,512]{3,2,1,0:T(8,128)S(1)}, f32[5,1,24,512]{3,2,1,0:T(8,128)S(1)}, u32[]{:S(2)}, u32[]{:S(2)}) collective-permute-start(f32[5,1,24,512]{3,2,1,0:T(8,128)S(1)} %get-tuple-element.60), channel_id=1, source_target_pairs={{16,0},{32,16},{48,32},{64,48},{80,64},{96,80},{112,96},{128,112},... | collective-permute-start | bytes 737288 | tf_op jit(solution)/shard_map/ppermute | solution.py:304
  12.7 1.3 %collective-permute-start.1 = (f32[5,1,24,512]{3,2,1,0:T(8,128)S(1)}, f32[5,1,24,512]{3,2,1,0:T(8,128)S(1)}, u32[]{:S(2)}, u32[]{:S(2)}) collective-permute-start(f32[5,1,24,512]{3,2,1,0:T(8,128)S(1)} %get-tuple-element.61), channel_id=1, source_target_pairs={{0,16},{16,32},{32,48},{48,64},{64,80},{80,96},{96,112},{112,128},... | collective-permute-start | bytes 737288 | tf_op jit(solution)/shard_map/ppermute | solution.py:301
  14.0 1.6 %collective-permute-start = (f32[5,1,32,512]{3,2,1,0:T(8,128)S(1)}, f32[5,1,32,512]{3,2,1,0:T(8,128)S(1)}, u32[]{:S(2)}, u32[]{:S(2)}) collective-permute-start(f32[5,1,32,512]{3,2,1,0:T(8,128)S(1)} %get-tuple-element.35), channel_id=1, source_target_pairs={{0,6},{2,8},{4,10},{6,12},{8,14},{10,0},{12,2},{14,4},{1,7},{3,9},... | collective-permute-start | bytes 983048 | tf_op jit(solution)/shard_map/ppermute | solution.py:298
  15.6 2.8 %collective-permute-start.9 = (f32[5,1,32,512]{3,2,1,0:T(8,128)S(1)}, f32[5,1,32,512]{3,2,1,0:T(8,128)S(1)}, u32[]{:S(2)}, u32[]{:S(2)}) collective-permute-start(f32[5,1,32,512]{3,2,1,0:T(8,128)S(1)} %get-tuple-element.55), channel_id=1, source_target_pairs={{0,10},{2,12},{4,14},{6,0},{8,2},{10,4},{12,6},{14,8},{1,11},{3,13... | collective-permute-start | bytes 983048 | tf_op jit(solution)/shard_map/ppermute | solution.py:298
  18.5 1.4 %shard_map.88 = (f32[5,1,32,512]{3,2,1,0:T(8,128)S(1)}, f32[5,1,32,512]{3,2,1,0:T(8,128)S(1)}, f32[3,1,32,512]{3,2,1,0:T(8,128)S(1)}, f32[3,1,32,512]{3,2,1,0:T(...) custom-call(f32[5,1,256,512]{3,2,1,0:T(8,128)} %cells), custom_call_target="tpu_custom_call" | custom-call | bytes 4587520 | tf_op jit(solution)/shard_map/pallas_call | solution.py:260
  19.9 0.0 collective-permute-done.3.refs_1_
  19.9 0.0 copy-start.1
  19.9 0.0 copy-start.2
  19.9 0.0 copy-start.3
  19.9 0.0 copy-start.4
  19.9 0.0 copy-start.5
  20.0 0.0 copy-start.6
  20.0 8.7 %collective-permute-start.6 = (f32[5,1,32,512]{3,2,1,0:T(8,128)S(1)}, f32[5,1,32,512]{3,2,1,0:T(8,128)S(1)}, u32[]{:S(2)}, u32[]{:S(2)}) collective-permute-start(f32[5,1,32,512]{3,2,1,0:T(8,128)S(1)} %get-tuple-element.50), channel_id=1, source_target_pairs={{0,12},{2,14},{4,0},{6,2},{8,4},{10,6},{12,8},{14,10},{1,13},{3,15... | collective-permute-start | bytes 983048 | tf_op jit(solution)/shard_map/ppermute | solution.py:298
  28.6 0.0 collective-permute-done.1.below
  28.6 0.9 %collective-permute-start.4 = (f32[5,1,32,512]{3,2,1,0:T(8,128)S(1)}, f32[5,1,32,512]{3,2,1,0:T(8,128)S(1)}, u32[]{:S(2)}, u32[]{:S(2)}) collective-permute-start(f32[5,1,32,512]{3,2,1,0:T(8,128)S(1)} %get-tuple-element.41), channel_id=1, source_target_pairs={{0,4},{2,6},{4,8},{6,10},{8,12},{10,14},{12,0},{14,2},{1,5},{3,7},... | collective-permute-start | bytes 983048 | tf_op jit(solution)/shard_map/ppermute | solution.py:298
  29.5 5.3 %shard_map.89 = f32[5,1,256,512]{3,2,1,0:T(8,128)} custom-call(f32[5,1,256,512]{3,2,1,0:T(8,128)S(1)} %copy-done, f32[5,1,24,512]{3,2,1,0:T(8,128)S(1)} %collective-permute-done.1.below, f32[5,1,24,512]{3,2,1,0:T(8,128)S(1)} %collective-permute-done.2.above), custom_call_target="tpu_custom_call" | custom-call | flops 13107200 | bytes 5242880 | tf_op jit(solution)/shard_map/pallas_call | solution.py:306
  34.9 15.6 %collective-permute-done.refs_2_ = f32[5,1,32,512]{3,2,1,0:T(8,128)S(1)} collective-permute-done((f32[5,1,32,512]{3,2,1,0:T(8,128)S(1)}, f32[5,1,32,512]{3,2,1,0:T(8,128)S(1)}, u32[]{:S(2)}, u32[]{:S(2)}) %collective-permute-start) | collective-permute-done | bytes 327712 | tf_op jit(solution)/shard_map/ppermute | solution.py:298
  50.5 0.0 collective-permute-done.9.refs_0_.refs_1_
  50.5 1.5 %collective-permute-start.8 = (f32[3,1,32,512]{3,2,1,0:T(8,128)S(1)}, f32[3,1,32,512]{3,2,1,0:T(8,128)S(1)}, u32[]{:S(2)}, u32[]{:S(2)}) collective-permute-start(f32[3,1,32,512]{3,2,1,0:T(8,128)S(1)} %get-tuple-element.53), channel_id=1, source_target_pairs={{0,2},{2,4},{4,6},{6,8},{8,10},{10,12},{12,14},{14,0},{1,3},{3,5},... | collective-permute-start | bytes 589832 | tf_op jit(solution)/shard_map/ppermute | solution.py:298
  52.0 0.0 collective-permute-start.5
  52.0 2.2 %shard_map.90.refs_10_ = f32[5,1,32,4096]{3,2,1,0:T(8,128)} custom-call(f32[5,1,32,512]{3,2,1,0:T(8,128)S(1)} %collective-permute-done.9.refs_0_.refs_1_, f32[5,1,32,512]{3,2,1,0:T(8,128)S(1)} %collective-permute-done.3.refs_1_, f32[5,1,32,512]{3,2,1,0:T(8,128)S(1)} %collective-permute-done.refs_2_, f32[5,1,32,512]{3,2,1,0:T(8,128)S(1)} %get-tuple-element.45.refs_3_.refs_2_, ...), custom_call_target="tpu_custom_call" | custom-call | flops 1132462080 | bytes 1966080 | tf_op jit(solution)/shard_map/pallas_call | solution.py:211
  54.2 6.0 %collective-permute-done.6.refs_0_.refs_4_ = f32[5,1,32,512]{3,2,1,0:T(8,128)S(1)} collective-permute-done((f32[5,1,32,512]{3,2,1,0:T(8,128)S(1)}, f32[5,1,32,512]{3,2,1,0:T(8,128)S(1)}, u32[]{:S(2)}, u32[]{:S(2)}) %collective-permute-start.6) | collective-permute-done | bytes 327712 | tf_op jit(solution)/shard_map/ppermute | solution.py:298
  60.2 1.8 %shard_map.91.refs_11_ = f32[5,1,32,4096]{3,2,1,0:T(8,128)} custom-call(f32[5,1,32,512]{3,2,1,0:T(8,128)S(1)} %collective-permute-done.6.refs_0_.refs_4_, f32[5,1,32,512]{3,2,1,0:T(8,128)S(1)} %collective-permute-done.9.refs_0_.refs_1_, f32[5,1,32,512]{3,2,1,0:T(8,128)S(1)} %collective-permute-done.refs_2_, ...), custom_call_target="tpu_custom_call", output_to_operand_aliasing={{}: (10, {})} | custom-call | flops 754974720 | bytes 1310720 | tf_op jit(solution)/shard_map/pallas_call | solution.py:211
  62.0 1.9 %collective-permute-done.10.refs_3_ = f32[3,1,32,512]{3,2,1,0:T(8,128)S(1)} collective-permute-done((f32[3,1,32,512]{3,2,1,0:T(8,128)S(1)}, f32[3,1,32,512]{3,2,1,0:T(8,128)S(1)}, u32[]{:S(2)}, u32[]{:S(2)}) %collective-permute-start.10) | collective-permute-done | bytes 196640 | tf_op jit(solution)/shard_map/ppermute | solution.py:298
  64.0 1.7 %shard_map.92.refs_11_ = f32[5,1,32,4096]{3,2,1,0:T(8,128)} custom-call(f32[5,1,32,512]{3,2,1,0:T(8,128)S(1)} %collective-permute-done.4.refs_3_.refs_0_, f32[3,1,32,512]{3,2,1,0:T(8,128)S(1)} %collective-permute-done.8.refs_1_, f32[5,1,32,512]{3,2,1,0:T(8,128)S(1)} %get-tuple-element.45.refs_3_.refs_2_, ...), custom_call_target="tpu_custom_call", output_to_operand_aliasing={{}: (11, {})} | custom-call | flops 679477248 | bytes 1179648 | tf_op jit(solution)/shard_map/pallas_call | solution.py:211
  65.7 1.1 %collective-permute-done.7.refs_3_ = f32[2,1,32,512]{3,2,1,0:T(8,128)S(1)} collective-permute-done((f32[2,1,32,512]{3,2,1,0:T(8,128)S(1)}, f32[2,1,32,512]{3,2,1,0:T(8,128)S(1)}, u32[]{:S(2)}, u32[]{:S(2)}) %collective-permute-start.7) | collective-permute-done | bytes 131104 | tf_op jit(solution)/shard_map/ppermute | solution.py:298
  66.8 1.4 %shard_map.93 = f32[5,1,32,4096]{3,2,1,0:T(8,128)} custom-call(f32[5,1,32,512]{3,2,1,0:T(8,128)S(1)} %collective-permute-done.4.refs_3_.refs_0_, f32[2,1,32,512]{3,2,1,0:T(8,128)S(1)} %collective-permute-done.5.refs_1_, f32[5,1,32,512]{3,2,1,0:T(8,128)S(1)} %get-tuple-element.45.refs_3_.refs_2_, ...), custom_call_target="tpu_custom_call", output_to_operand_aliasing={{}: (11, {})} | custom-call | flops 452984832 | bytes 786432 | tf_op jit(solution)/shard_map/pallas_call | solution.py:211
  (13 shorter events, 0.0 us)
Async XLA Ops:
  1.6 27.9 %copy-start = (f32[5,1,256,512]{3,2,1,0:T(8,128)S(1)}, f32[5,1,256,512]{3,2,1,0:T(8,128)}, u32[]{:S(2)}) copy-start(f32[5,1,256,512]{3,2,1,0:T(8,128)} %cells) | copy-start | bytes 7864324
  1.6 18.2 %collective-permute-start.3 = (f32[5,1,32,512]{3,2,1,0:T(8,128)S(1)}, f32[5,1,32,512]{3,2,1,0:T(8,128)S(1)}, u32[]{:S(2)}, u32[]{:S(2)}) collective-permute-start(f32[5,1,32,512]{3,2,1,0:T(8,128)S(1)} %shard_map.86), channel_id=1, source_target_pairs={{0,8},{2,10},{4,12},{6,14},{8,0},{10,2},{12,4},{14,6},{1,9},{3,11}... | collective-permute-start | bytes 983048 | tf_op jit(solution)/shard_map/ppermute | solution.py:298
  11.7 8.3 %collective-permute-start.2 = (f32[5,1,24,512]{3,2,1,0:T(8,128)S(1)}, f32[5,1,24,512]{3,2,1,0:T(8,128)S(1)}, u32[]{:S(2)}, u32[]{:S(2)}) collective-permute-start(f32[5,1,24,512]{3,2,1,0:T(8,128)S(1)} %get-tuple-element.60), channel_id=1, source_target_pairs={{16,0},{32,16},{48,32},{64,48},{80,64},{96,80},{112,96},{128,112},... | collective-permute-start | bytes 737288 | tf_op jit(solution)/shard_map/ppermute | solution.py:304
  12.7 15.9 %collective-permute-start.1 = (f32[5,1,24,512]{3,2,1,0:T(8,128)S(1)}, f32[5,1,24,512]{3,2,1,0:T(8,128)S(1)}, u32[]{:S(2)}, u32[]{:S(2)}) collective-permute-start(f32[5,1,24,512]{3,2,1,0:T(8,128)S(1)} %get-tuple-element.61), channel_id=1, source_target_pairs={{0,16},{16,32},{32,48},{48,64},{64,80},{80,96},{96,112},{112,128},... | collective-permute-start | bytes 737288 | tf_op jit(solution)/shard_map/ppermute | solution.py:301
  14.0 36.5 %collective-permute-start = (f32[5,1,32,512]{3,2,1,0:T(8,128)S(1)}, f32[5,1,32,512]{3,2,1,0:T(8,128)S(1)}, u32[]{:S(2)}, u32[]{:S(2)}) collective-permute-start(f32[5,1,32,512]{3,2,1,0:T(8,128)S(1)} %get-tuple-element.35), channel_id=1, source_target_pairs={{0,6},{2,8},{4,10},{6,12},{8,14},{10,0},{12,2},{14,4},{1,7},{3,9},... | collective-permute-start | bytes 983048 | tf_op jit(solution)/shard_map/ppermute | solution.py:298
  15.6 34.9 %collective-permute-start.9 = (f32[5,1,32,512]{3,2,1,0:T(8,128)S(1)}, f32[5,1,32,512]{3,2,1,0:T(8,128)S(1)}, u32[]{:S(2)}, u32[]{:S(2)}) collective-permute-start(f32[5,1,32,512]{3,2,1,0:T(8,128)S(1)} %get-tuple-element.55), channel_id=1, source_target_pairs={{0,10},{2,12},{4,14},{6,0},{8,2},{10,4},{12,6},{14,8},{1,11},{3,13... | collective-permute-start | bytes 983048 | tf_op jit(solution)/shard_map/ppermute | solution.py:298
  19.9 32.1 %copy-start.1 = (bf16[256,256]{1,0:T(8,128)(2,1)S(1)}, bf16[256,256]{1,0:T(8,128)(2,1)}, u32[]{:S(2)}) copy-start(bf16[256,256]{1,0:T(8,128)(2,1)} %constant.17.clone.refs_9_.refs_10_) | copy-start | bytes 393220
  19.9 32.1 %copy-start.2 = (bf16[256,256]{1,0:T(8,128)(2,1)S(1)}, bf16[256,256]{1,0:T(8,128)(2,1)}, u32[]{:S(2)}) copy-start(bf16[256,256]{1,0:T(8,128)(2,1)} %constant.16.clone.refs_8_.refs_9_) | copy-start | bytes 393220
  19.9 32.1 %copy-start.3 = (bf16[256,256]{1,0:T(8,128)(2,1)S(1)}, bf16[256,256]{1,0:T(8,128)(2,1)}, u32[]{:S(2)}) copy-start(bf16[256,256]{1,0:T(8,128)(2,1)} %constant.15.clone.refs_7_.refs_8_) | copy-start | bytes 393220
  19.9 32.1 %copy-start.4 = (bf16[256,256]{1,0:T(8,128)(2,1)S(1)}, bf16[256,256]{1,0:T(8,128)(2,1)}, u32[]{:S(2)}) copy-start(bf16[256,256]{1,0:T(8,128)(2,1)} %constant.14.clone.refs_6_.refs_7_) | copy-start | bytes 393220
  19.9 32.1 %copy-start.5 = (bf16[256,256]{1,0:T(8,128)(2,1)S(1)}, bf16[256,256]{1,0:T(8,128)(2,1)}, u32[]{:S(2)}) copy-start(bf16[256,256]{1,0:T(8,128)(2,1)} %constant.13.clone.refs_5_.refs_6_) | copy-start | bytes 393220
  20.0 32.1 %copy-start.6 = (bf16[256,256]{1,0:T(8,128)(2,1)S(1)}, bf16[256,256]{1,0:T(8,128)(2,1)}, u32[]{:S(2)}) copy-start(bf16[256,256]{1,0:T(8,128)(2,1)} %constant.12.clone.refs_4_.refs_5_) | copy-start | bytes 393220
  20.0 40.2 %collective-permute-start.6 = (f32[5,1,32,512]{3,2,1,0:T(8,128)S(1)}, f32[5,1,32,512]{3,2,1,0:T(8,128)S(1)}, u32[]{:S(2)}, u32[]{:S(2)}) collective-permute-start(f32[5,1,32,512]{3,2,1,0:T(8,128)S(1)} %get-tuple-element.50), channel_id=1, source_target_pairs={{0,12},{2,14},{4,0},{6,2},{8,4},{10,6},{12,8},{14,10},{1,13},{3,15... | collective-permute-start | bytes 983048 | tf_op jit(solution)/shard_map/ppermute | solution.py:298
  28.6 31.6 %collective-permute-start.4 = (f32[5,1,32,512]{3,2,1,0:T(8,128)S(1)}, f32[5,1,32,512]{3,2,1,0:T(8,128)S(1)}, u32[]{:S(2)}, u32[]{:S(2)}) collective-permute-start(f32[5,1,32,512]{3,2,1,0:T(8,128)S(1)} %get-tuple-element.41), channel_id=1, source_target_pairs={{0,4},{2,6},{4,8},{6,10},{8,12},{10,14},{12,0},{14,2},{1,5},{3,7},... | collective-permute-start | bytes 983048 | tf_op jit(solution)/shard_map/ppermute | solution.py:298
  50.5 13.5 %collective-permute-start.10 = (f32[3,1,32,512]{3,2,1,0:T(8,128)S(1)}, f32[3,1,32,512]{3,2,1,0:T(8,128)S(1)}, u32[]{:S(2)}, u32[]{:S(2)}) collective-permute-start(f32[3,1,32,512]{3,2,1,0:T(8,128)S(1)} %get-tuple-element.56), channel_id=1, source_target_pairs={{0,14},{2,0},{4,2},{6,4},{8,6},{10,8},{12,10},{14,12},{1,15},{3,1}... | collective-permute-start | bytes 589832 | tf_op jit(solution)/shard_map/ppermute | solution.py:298
  50.5 13.5 %collective-permute-start.8 = (f32[3,1,32,512]{3,2,1,0:T(8,128)S(1)}, f32[3,1,32,512]{3,2,1,0:T(8,128)S(1)}, u32[]{:S(2)}, u32[]{:S(2)}) collective-permute-start(f32[3,1,32,512]{3,2,1,0:T(8,128)S(1)} %get-tuple-element.53), channel_id=1, source_target_pairs={{0,2},{2,4},{4,6},{6,8},{8,10},{10,12},{12,14},{14,0},{1,3},{3,5},... | collective-permute-start | bytes 589832 | tf_op jit(solution)/shard_map/ppermute | solution.py:298
  52.0 13.7 %collective-permute-start.5 = (f32[2,1,32,512]{3,2,1,0:T(8,128)S(1)}, f32[2,1,32,512]{3,2,1,0:T(8,128)S(1)}, u32[]{:S(2)}, u32[]{:S(2)}) collective-permute-start(f32[2,1,32,512]{3,2,1,0:T(8,128)S(1)} %get-tuple-element.44), channel_id=1, source_target_pairs={{0,2},{2,4},{4,6},{6,8},{8,10},{10,12},{12,14},{14,0},{1,3},{3,5},... | collective-permute-start | bytes 393224 | tf_op jit(solution)/shard_map/ppermute | solution.py:298
  60.2 6.6 %collective-permute-start.7 = (f32[2,1,32,512]{3,2,1,0:T(8,128)S(1)}, f32[2,1,32,512]{3,2,1,0:T(8,128)S(1)}, u32[]{:S(2)}, u32[]{:S(2)}) collective-permute-start(f32[2,1,32,512]{3,2,1,0:T(8,128)S(1)} %get-tuple-element.51), channel_id=1, source_target_pairs={{0,14},{2,0},{4,2},{6,4},{8,6},{10,8},{12,10},{14,12},{1,15},{3,1}... | collective-permute-start | bytes 393224 | tf_op jit(solution)/shard_map/ppermute | solution.py:298

commit v4 on v3

--- a/solution.py
+++ b/solution.py
@@ -9,20 +9,20 @@
 LEVELS = 4
 HALO = 24
 LIMIT = 8 * 2**20
-STACK = 400
+STACK = 640
 STEPS = (
     ("y4", ()),
+    ("y3", ()),
+    ("y5", ()),
     ("b", ()),
     ("a", ()),
     ("X", ()),
-    ("y3", ()),
-    ("y5", ()),
-    ("y2", ("y4", "b", )),
-    ("y6", ("y4", "a", )),
-    ("y1p", ("y3", "X", )),
-    ("y7p", ("y5", )),
-    ("y1q", ("y3", )),
-    ("y7q", ("y6", )),
+    ("y6", ("y4", "b", )),
+    ("y2", ("y4", "a", )),
+    ("y7p", ("y3", "X", )),
+    ("y1p", ("y5", )),
+    ("y7q", ("y3", )),
+    ("y1q", ("y5", )),
     ("A", ()),
     ("B", ()),
     ("C", ()),
@@ -133,7 +133,6 @@
 
 
 FULL = ((2, 0), (0, 2), (1, 1), (1, 0), (0, 1), (0, 0))
-SHORT = ((1, 0), (0, 1), (0, 0))
 
 
 def y_kernel(count, places, starts, first_field, fields, spans, aliased):
@@ -182,8 +181,8 @@
         for start in range(0, len(units), together):
             group = units[start : start + together]
             middle = [stacked((0, LANES), t, group) for t in range(3)]
-            sides = [stacked((-LANES, UNIT), t, group) for t in range(2)]
-            solved = product(sides, outer, SHORT) + product(middle, inner, FULL)
+            sides = [stacked((-LANES, UNIT), t, group) for t in range(3)]
+            solved = product(sides, outer, FULL) + product(middle, inner, FULL)
             for number, (lane, at, first, last, _) in enumerate(group):
                 part = solved[number * size : (number + 1) * size]
                 result[:, 0, :, at : at + UNIT] = part.reshape(fields, rows, UNIT)
@@ -220,7 +219,7 @@
         input_output_aliases={len(operands): 0} if aliased else {},
         compiler_params=pltpu.CompilerParams(vmem_limit_bytes=LIMIT),
         cost_estimate=pl.CostEstimate(
-            flops=9 * 2 * 256 * size, bytes_accessed=8 * size, transcendentals=0
+            flops=12 * 2 * 256 * size, bytes_accessed=8 * size, transcendentals=0
         ),
     )(*[pltpu.with_memory_space_constraint(x, pltpu.VMEM) for x in operands], *([partial] if aliased else []))
 
@@ -279,6 +278,7 @@
     ring_2 = ((2 * c + e, 3 * c + e), (6 * c - e, 7 * c - e))
     ring_1 = ((7 * c - e, 8 * c + e), (9 * c - e, 10 * c + e))
     plans = {
+        "E": ([2, 3, 4, 5, 6, 0], ((2 * c + e, 7 * c - e), (8 * c + e, 9 * c - e)), ""),
         "A": ([3, 4, 5, 0], inner, ""),
         "B": ([2, 3, 5, 6], ring_2, ""),
         "C": ([6, 7, 0, 1, 2], ring_1, "p" if SPLIT else ""),

time: 68.3 us -> 69.2 us (1.013)
  waiting for transfers between devices: 24.7 us -> 23.5 us
  starting transfers between devices: 25.7 us -> 26.8 us
  Pallas kernels: 15.9 us -> 16.7 us
    ppermute x9, starting transfers between devices: 23.3 us -> 24.6 us  [body(): lax.ppermute(cut, 'gy', [(i, (i + hop) % count) for i in range(count)])]
    ppermute x9, waiting for transfers between devices: 24.6 us -> 23.5 us  [body(): lax.ppermute(cut, 'gy', [(i, (i + hop) % count) for i in range(count)])]
    ppermute x1, starting transfers between devices: 1.03 us -> 0.01 us  [body(): lax.ppermute(halo, 'gx', [((i + 1) % ring, i) for i in range(ring)])]
    ppermute x1, starting transfers between devices: 1.27 us -> 2.21 us  [body(): lax.ppermute(halo, 'gx', [(i, (i + 1) % ring) for i in range(ring)])]
    pallas_call x4, Pallas kernels: 7.05 us -> 7.88 us  [y_call(): pl.pallas_call(y_kernel(count, places, starts, first_field, fields, spans...]
  transfers between devices with their start and end apart: 11 -> 11, of which waited for: 4 -> 4; matrix products, arithmetic and copies ran while one was open for 2% -> 2% of each run, Pallas kernels for 20% -> 21%
where the time goes in v4:
time: 69.2 us; the launch traced here: 69 us
  starting transfers between devices  26.8 us (39%)
  waiting for transfers between devices  23.5 us (34%)
  Pallas kernels  16.7 us (24%)
  local copies, waits for them, and re-layouts  1.15 us (2%)
  between operations  0.8 us (1%)
    ppermute x9, starting transfers between devices, body(): lax.ppermute(cut, 'gy', [(i, (i + hop) % count) for i in range(count)])  24.6 us
    ppermute x9, waiting for transfers between devices, body(): lax.ppermute(cut, 'gy', [(i, (i + hop) % count) for i in range(count)])  23.5 us
    pallas_call x4, Pallas kernels, y_call(): pl.pallas_call(y_kernel(count, places, starts, first_field, fields, spans...  7.88 us
    pallas_call x1, Pallas kernels, body(): pl.pallas_call(x_kernel, out_shape=jax.ShapeDtypeStruct(fields.shape, fie...  5.33 us
    pallas_call x3, Pallas kernels, body(): pl.pallas_call(cut_kernel(count, pieces), out_shape=[jax.ShapeDtypeStruct...  3.51 us
    ppermute x1, starting transfers between devices, body(): lax.ppermute(halo, 'gx', [(i, (i + 1) % ring) for i in range(ring)])  2.21 us
  transfers between devices with their start and end apart: 11, of which 4 were waited for; matrix products, arithmetic and copies ran while one was open for 2% of the time, Pallas kernels for 21%

profile of v4, /device:TPU:1, one launch (start us, length us, event | category | flops | bytes accessed | tf_op | source)
XLA Modules:
  0.0 69.0 jit_solution(16519006404267544339)
XLA Ops:
  0.6 1.0 %shard_map.86 = f32[5,1,32,512]{3,2,1,0:T(8,128)S(1)} custom-call(f32[5,1,256,512]{3,2,1,0:T(8,128)} %cells), custom_call_target="tpu_custom_call" | custom-call | bytes 655360 | tf_op jit(solution)/shard_map/pallas_call | solution.py:259
  1.6 0.0 copy-start
  1.6 7.8 %collective-permute-start.3 = (f32[5,1,32,512]{3,2,1,0:T(8,128)S(1)}, f32[5,1,32,512]{3,2,1,0:T(8,128)S(1)}, u32[]{:S(2)}, u32[]{:S(2)}) collective-permute-start(f32[5,1,32,512]{3,2,1,0:T(8,128)S(1)} %shard_map.86), channel_id=1, source_target_pairs={{0,8},{2,10},{4,12},{6,14},{8,0},{10,2},{12,4},{14,6},{1,9},{3,11}... | collective-permute-start | bytes 983048 | tf_op jit(solution)/shard_map/ppermute | solution.py:298
  9.5 1.1 %shard_map.87 = (f32[5,1,32,512]{3,2,1,0:T(8,128)S(1)}, f32[5,1,32,512]{3,2,1,0:T(8,128)S(1)}) custom-call(f32[5,1,256,512]{3,2,1,0:T(8,128)} %cells), custom_call_target="tpu_custom_call" | custom-call | bytes 1310720 | tf_op jit(solution)/shard_map/pallas_call | solution.py:259
  10.6 1.1 %fusion = (f32[5,1,24,512]{3,2,1,0:T(8,128)S(1)}, f32[5,1,24,512]{3,2,1,0:T(8,128)S(1)}) fusion(f32[5,1,256,512]{3,2,1,0:T(8,128)} %cells), kind=kLoop, calls=%fused_computation | loop fusion | bytes 983040 | tf_op jit(solution)/shard_map/slice | solution.py:303
  11.7 2.2 %collective-permute-start.1 = (f32[5,1,24,512]{3,2,1,0:T(8,128)S(1)}, f32[5,1,24,512]{3,2,1,0:T(8,128)S(1)}, u32[]{:S(2)}, u32[]{:S(2)}) collective-permute-start(f32[5,1,24,512]{3,2,1,0:T(8,128)S(1)} %get-tuple-element.61), channel_id=1, source_target_pairs={{0,16},{16,32},{32,48},{48,64},{64,80},{80,96},{96,112},{112,128},... | collective-permute-start | bytes 737288 | tf_op jit(solution)/shard_map/ppermute | solution.py:301
  13.9 0.0 collective-permute-start.2
  13.9 1.6 %collective-permute-start = (f32[5,1,32,512]{3,2,1,0:T(8,128)S(1)}, f32[5,1,32,512]{3,2,1,0:T(8,128)S(1)}, u32[]{:S(2)}, u32[]{:S(2)}) collective-permute-start(f32[5,1,32,512]{3,2,1,0:T(8,128)S(1)} %get-tuple-element.35), channel_id=1, source_target_pairs={{0,6},{2,8},{4,10},{6,12},{8,14},{10,0},{12,2},{14,4},{1,7},{3,9},... | collective-permute-start | bytes 983048 | tf_op jit(solution)/shard_map/ppermute | solution.py:298
  15.5 2.8 %collective-permute-start.5 = (f32[5,1,32,512]{3,2,1,0:T(8,128)S(1)}, f32[5,1,32,512]{3,2,1,0:T(8,128)S(1)}, u32[]{:S(2)}, u32[]{:S(2)}) collective-permute-start(f32[5,1,32,512]{3,2,1,0:T(8,128)S(1)} %get-tuple-element.46), channel_id=1, source_target_pairs={{0,10},{2,12},{4,14},{6,0},{8,2},{10,4},{12,6},{14,8},{1,11},{3,13... | collective-permute-start | bytes 983048 | tf_op jit(solution)/shard_map/ppermute | solution.py:298
  18.4 1.4 %shard_map.88 = (f32[5,1,32,512]{3,2,1,0:T(8,128)S(1)}, f32[5,1,32,512]{3,2,1,0:T(8,128)S(1)}, f32[3,1,32,512]{3,2,1,0:T(8,128)S(1)}, f32[3,1,32,512]{3,2,1,0:T(...) custom-call(f32[5,1,256,512]{3,2,1,0:T(8,128)} %cells), custom_call_target="tpu_custom_call" | custom-call | bytes 4587520 | tf_op jit(solution)/shard_map/pallas_call | solution.py:259
  19.8 0.0 collective-permute-done.3.refs_1_
  19.8 0.0 copy-start.1
  19.8 0.0 copy-start.2
  19.8 0.0 copy-start.3
  19.8 0.0 copy-start.4
  19.9 0.0 copy-start.5
  19.9 0.0 copy-start.6
  19.9 0.0 collective-permute-done.1.below
  19.9 8.7 %collective-permute-start.8 = (f32[5,1,32,512]{3,2,1,0:T(8,128)S(1)}, f32[5,1,32,512]{3,2,1,0:T(8,128)S(1)}, u32[]{:S(2)}, u32[]{:S(2)}) collective-permute-start(f32[5,1,32,512]{3,2,1,0:T(8,128)S(1)} %get-tuple-element.54), channel_id=1, source_target_pairs={{0,12},{2,14},{4,0},{6,2},{8,4},{10,6},{12,8},{14,10},{1,13},{3,15... | collective-permute-start | bytes 983048 | tf_op jit(solution)/shard_map/ppermute | solution.py:298
  28.6 0.9 %collective-permute-start.4 = (f32[5,1,32,512]{3,2,1,0:T(8,128)S(1)}, f32[5,1,32,512]{3,2,1,0:T(8,128)S(1)}, u32[]{:S(2)}, u32[]{:S(2)}) collective-permute-start(f32[5,1,32,512]{3,2,1,0:T(8,128)S(1)} %get-tuple-element.43), channel_id=1, source_target_pairs={{0,4},{2,6},{4,8},{6,10},{8,12},{10,14},{12,0},{14,2},{1,5},{3,7},... | collective-permute-start | bytes 983048 | tf_op jit(solution)/shard_map/ppermute | solution.py:298
  29.5 5.3 %shard_map.89 = f32[5,1,256,512]{3,2,1,0:T(8,128)} custom-call(f32[5,1,256,512]{3,2,1,0:T(8,128)S(1)} %copy-done, f32[5,1,24,512]{3,2,1,0:T(8,128)S(1)} %collective-permute-done.1.below, f32[5,1,24,512]{3,2,1,0:T(8,128)S(1)} %collective-permute-done.2.above), custom_call_target="tpu_custom_call" | custom-call | flops 13107200 | bytes 5242880 | tf_op jit(solution)/shard_map/pallas_call | solution.py:306
  34.8 15.6 %collective-permute-done.refs_2_ = f32[5,1,32,512]{3,2,1,0:T(8,128)S(1)} collective-permute-done((f32[5,1,32,512]{3,2,1,0:T(8,128)S(1)}, f32[5,1,32,512]{3,2,1,0:T(8,128)S(1)}, u32[]{:S(2)}, u32[]{:S(2)}) %collective-permute-start) | collective-permute-done | bytes 327712 | tf_op jit(solution)/shard_map/ppermute | solution.py:298
  50.4 0.0 collective-permute-done.5.refs_0_.refs_1_
  50.4 0.0 collective-permute-start.6
  50.4 2.7 %collective-permute-start.10 = (f32[3,1,32,512]{3,2,1,0:T(8,128)S(1)}, f32[3,1,32,512]{3,2,1,0:T(8,128)S(1)}, u32[]{:S(2)}, u32[]{:S(2)}) collective-permute-start(f32[3,1,32,512]{3,2,1,0:T(8,128)S(1)} %get-tuple-element.56), channel_id=1, source_target_pairs={{0,14},{2,0},{4,2},{6,4},{8,6},{10,8},{12,10},{14,12},{1,15},{3,1}... | collective-permute-start | bytes 589832 | tf_op jit(solution)/shard_map/ppermute | solution.py:298
  53.2 2.6 %shard_map.90.refs_10_ = f32[5,1,32,4096]{3,2,1,0:T(8,128)} custom-call(f32[5,1,32,512]{3,2,1,0:T(8,128)S(1)} %collective-permute-done.5.refs_0_.refs_1_, f32[5,1,32,512]{3,2,1,0:T(8,128)S(1)} %collective-permute-done.3.refs_1_, f32[5,1,32,512]{3,2,1,0:T(8,128)S(1)} %collective-permute-done.refs_2_, f32[5,1,32,512]{3,2,1,0:T(8,128)S(1)} %get-tuple-element.49.refs_3_.refs_2_, ...), custom_call_target="tpu_custom_call" | custom-call | flops 1509949440 | bytes 1966080 | tf_op jit(solution)/shard_map/pallas_call | solution.py:210
  55.8 4.5 %collective-permute-done.8.refs_0_.refs_4_ = f32[5,1,32,512]{3,2,1,0:T(8,128)S(1)} collective-permute-done((f32[5,1,32,512]{3,2,1,0:T(8,128)S(1)}, f32[5,1,32,512]{3,2,1,0:T(8,128)S(1)}, u32[]{:S(2)}, u32[]{:S(2)}) %collective-permute-start.8) | collective-permute-done | bytes 327712 | tf_op jit(solution)/shard_map/ppermute | solution.py:298
  60.3 2.0 %shard_map.91.refs_11_ = f32[5,1,32,4096]{3,2,1,0:T(8,128)} custom-call(f32[5,1,32,512]{3,2,1,0:T(8,128)S(1)} %collective-permute-done.8.refs_0_.refs_4_, f32[5,1,32,512]{3,2,1,0:T(8,128)S(1)} %collective-permute-done.5.refs_0_.refs_1_, f32[5,1,32,512]{3,2,1,0:T(8,128)S(1)} %collective-permute-done.refs_2_, ...), custom_call_target="tpu_custom_call", output_to_operand_aliasing={{}: (10, {})} | custom-call | flops 1006632960 | bytes 1310720 | tf_op jit(solution)/shard_map/pallas_call | solution.py:210
  62.3 2.7 %collective-permute-done.9.refs_1_ = f32[3,1,32,512]{3,2,1,0:T(8,128)S(1)} collective-permute-done((f32[3,1,32,512]{3,2,1,0:T(8,128)S(1)}, f32[3,1,32,512]{3,2,1,0:T(8,128)S(1)}, u32[]{:S(2)}, u32[]{:S(2)}) %collective-permute-start.9) | collective-permute-done | bytes 196640 | tf_op jit(solution)/shard_map/ppermute | solution.py:298
  65.0 1.8 %shard_map.92.refs_11_ = f32[5,1,32,4096]{3,2,1,0:T(8,128)} custom-call(f32[5,1,32,512]{3,2,1,0:T(8,128)S(1)} %collective-permute-done.4.refs_3_.refs_0_, f32[3,1,32,512]{3,2,1,0:T(8,128)S(1)} %collective-permute-done.9.refs_1_, f32[5,1,32,512]{3,2,1,0:T(8,128)S(1)} %get-tuple-element.49.refs_3_.refs_2_, ...), custom_call_target="tpu_custom_call", output_to_operand_aliasing={{}: (11, {})} | custom-call | flops 905969664 | bytes 1179648 | tf_op jit(solution)/shard_map/pallas_call | solution.py:210
  66.8 0.6 collective-permute-done.7.refs_3_
  67.5 1.5 %shard_map.93 = f32[5,1,32,4096]{3,2,1,0:T(8,128)} custom-call(f32[5,1,32,512]{3,2,1,0:T(8,128)S(1)} %collective-permute-done.4.refs_3_.refs_0_, f32[2,1,32,512]{3,2,1,0:T(8,128)S(1)} %collective-permute-done.6.refs_1_, f32[5,1,32,512]{3,2,1,0:T(8,128)S(1)} %get-tuple-element.49.refs_3_.refs_2_, ...), custom_call_target="tpu_custom_call", output_to_operand_aliasing={{}: (11, {})} | custom-call | flops 603979776 | bytes 786432 | tf_op jit(solution)/shard_map/pallas_call | solution.py:210
  (13 shorter events, 0.0 us)
Async XLA Ops:
  1.6 27.9 %copy-start = (f32[5,1,256,512]{3,2,1,0:T(8,128)S(1)}, f32[5,1,256,512]{3,2,1,0:T(8,128)}, u32[]{:S(2)}) copy-start(f32[5,1,256,512]{3,2,1,0:T(8,128)} %cells) | copy-start | bytes 7864324
  1.6 18.2 %collective-permute-start.3 = (f32[5,1,32,512]{3,2,1,0:T(8,128)S(1)}, f32[5,1,32,512]{3,2,1,0:T(8,128)S(1)}, u32[]{:S(2)}, u32[]{:S(2)}) collective-permute-start(f32[5,1,32,512]{3,2,1,0:T(8,128)S(1)} %shard_map.86), channel_id=1, source_target_pairs={{0,8},{2,10},{4,12},{6,14},{8,0},{10,2},{12,4},{14,6},{1,9},{3,11}... | collective-permute-start | bytes 983048 | tf_op jit(solution)/shard_map/ppermute | solution.py:298
  11.7 8.2 %collective-permute-start.1 = (f32[5,1,24,512]{3,2,1,0:T(8,128)S(1)}, f32[5,1,24,512]{3,2,1,0:T(8,128)S(1)}, u32[]{:S(2)}, u32[]{:S(2)}) collective-permute-start(f32[5,1,24,512]{3,2,1,0:T(8,128)S(1)} %get-tuple-element.61), channel_id=1, source_target_pairs={{0,16},{16,32},{32,48},{48,64},{64,80},{80,96},{96,112},{112,128},... | collective-permute-start | bytes 737288 | tf_op jit(solution)/shard_map/ppermute | solution.py:301
  13.9 14.8 %collective-permute-start.2 = (f32[5,1,24,512]{3,2,1,0:T(8,128)S(1)}, f32[5,1,24,512]{3,2,1,0:T(8,128)S(1)}, u32[]{:S(2)}, u32[]{:S(2)}) collective-permute-start(f32[5,1,24,512]{3,2,1,0:T(8,128)S(1)} %get-tuple-element.60), channel_id=1, source_target_pairs={{16,0},{32,16},{48,32},{64,48},{80,64},{96,80},{112,96},{128,112},... | collective-permute-start | bytes 737288 | tf_op jit(solution)/shard_map/ppermute | solution.py:304
  13.9 36.5 %collective-permute-start = (f32[5,1,32,512]{3,2,1,0:T(8,128)S(1)}, f32[5,1,32,512]{3,2,1,0:T(8,128)S(1)}, u32[]{:S(2)}, u32[]{:S(2)}) collective-permute-start(f32[5,1,32,512]{3,2,1,0:T(8,128)S(1)} %get-tuple-element.35), channel_id=1, source_target_pairs={{0,6},{2,8},{4,10},{6,12},{8,14},{10,0},{12,2},{14,4},{1,7},{3,9},... | collective-permute-start | bytes 983048 | tf_op jit(solution)/shard_map/ppermute | solution.py:298
  15.5 34.9 %collective-permute-start.5 = (f32[5,1,32,512]{3,2,1,0:T(8,128)S(1)}, f32[5,1,32,512]{3,2,1,0:T(8,128)S(1)}, u32[]{:S(2)}, u32[]{:S(2)}) collective-permute-start(f32[5,1,32,512]{3,2,1,0:T(8,128)S(1)} %get-tuple-element.46), channel_id=1, source_target_pairs={{0,10},{2,12},{4,14},{6,0},{8,2},{10,4},{12,6},{14,8},{1,11},{3,13... | collective-permute-start | bytes 983048 | tf_op jit(solution)/shard_map/ppermute | solution.py:298
  19.8 33.3 %copy-start.1 = (bf16[256,256]{1,0:T(8,128)(2,1)S(1)}, bf16[256,256]{1,0:T(8,128)(2,1)}, u32[]{:S(2)}) copy-start(bf16[256,256]{1,0:T(8,128)(2,1)} %constant.17.clone.refs_9_.refs_10_) | copy-start | bytes 393220
  19.8 33.3 %copy-start.2 = (bf16[256,256]{1,0:T(8,128)(2,1)S(1)}, bf16[256,256]{1,0:T(8,128)(2,1)}, u32[]{:S(2)}) copy-start(bf16[256,256]{1,0:T(8,128)(2,1)} %constant.16.clone.refs_8_.refs_9_) | copy-start | bytes 393220
  19.8 33.3 %copy-start.3 = (bf16[256,256]{1,0:T(8,128)(2,1)S(1)}, bf16[256,256]{1,0:T(8,128)(2,1)}, u32[]{:S(2)}) copy-start(bf16[256,256]{1,0:T(8,128)(2,1)} %constant.15.clone.refs_7_.refs_8_) | copy-start | bytes 393220
  19.8 33.3 %copy-start.4 = (bf16[256,256]{1,0:T(8,128)(2,1)S(1)}, bf16[256,256]{1,0:T(8,128)(2,1)}, u32[]{:S(2)}) copy-start(bf16[256,256]{1,0:T(8,128)(2,1)} %constant.14.clone.refs_6_.refs_7_) | copy-start | bytes 393220
  19.9 33.3 %copy-start.5 = (bf16[256,256]{1,0:T(8,128)(2,1)S(1)}, bf16[256,256]{1,0:T(8,128)(2,1)}, u32[]{:S(2)}) copy-start(bf16[256,256]{1,0:T(8,128)(2,1)} %constant.13.clone.refs_5_.refs_6_) | copy-start | bytes 393220
  19.9 33.3 %copy-start.6 = (bf16[256,256]{1,0:T(8,128)(2,1)S(1)}, bf16[256,256]{1,0:T(8,128)(2,1)}, u32[]{:S(2)}) copy-start(bf16[256,256]{1,0:T(8,128)(2,1)} %constant.12.clone.refs_4_.refs_5_) | copy-start | bytes 393220
  19.9 40.4 %collective-permute-start.8 = (f32[5,1,32,512]{3,2,1,0:T(8,128)S(1)}, f32[5,1,32,512]{3,2,1,0:T(8,128)S(1)}, u32[]{:S(2)}, u32[]{:S(2)}) collective-permute-start(f32[5,1,32,512]{3,2,1,0:T(8,128)S(1)} %get-tuple-element.54), channel_id=1, source_target_pairs={{0,12},{2,14},{4,0},{6,2},{8,4},{10,6},{12,8},{14,10},{1,13},{3,15... | collective-permute-start | bytes 983048 | tf_op jit(solution)/shard_map/ppermute | solution.py:298
  28.6 31.7 %collective-permute-start.4 = (f32[5,1,32,512]{3,2,1,0:T(8,128)S(1)}, f32[5,1,32,512]{3,2,1,0:T(8,128)S(1)}, u32[]{:S(2)}, u32[]{:S(2)}) collective-permute-start(f32[5,1,32,512]{3,2,1,0:T(8,128)S(1)} %get-tuple-element.43), channel_id=1, source_target_pairs={{0,4},{2,6},{4,8},{6,10},{8,12},{10,14},{12,0},{14,2},{1,5},{3,7},... | collective-permute-start | bytes 983048 | tf_op jit(solution)/shard_map/ppermute | solution.py:298
  50.4 16.4 %collective-permute-start.6 = (f32[2,1,32,512]{3,2,1,0:T(8,128)S(1)}, f32[2,1,32,512]{3,2,1,0:T(8,128)S(1)}, u32[]{:S(2)}, u32[]{:S(2)}) collective-permute-start(f32[2,1,32,512]{3,2,1,0:T(8,128)S(1)} %get-tuple-element.48), channel_id=1, source_target_pairs={{0,2},{2,4},{4,6},{6,8},{8,10},{10,12},{12,14},{14,0},{1,3},{3,5},... | collective-permute-start | bytes 393224 | tf_op jit(solution)/shard_map/ppermute | solution.py:298
  50.4 14.6 %collective-permute-start.9 = (f32[3,1,32,512]{3,2,1,0:T(8,128)S(1)}, f32[3,1,32,512]{3,2,1,0:T(8,128)S(1)}, u32[]{:S(2)}, u32[]{:S(2)}) collective-permute-start(f32[3,1,32,512]{3,2,1,0:T(8,128)S(1)} %get-tuple-element.55), channel_id=1, source_target_pairs={{0,2},{2,4},{4,6},{6,8},{8,10},{10,12},{12,14},{14,0},{1,3},{3,5},... | collective-permute-start | bytes 589832 | tf_op jit(solution)/shard_map/ppermute | solution.py:298
  50.4 14.6 %collective-permute-start.10 = (f32[3,1,32,512]{3,2,1,0:T(8,128)S(1)}, f32[3,1,32,512]{3,2,1,0:T(8,128)S(1)}, u32[]{:S(2)}, u32[]{:S(2)}) collective-permute-start(f32[3,1,32,512]{3,2,1,0:T(8,128)S(1)} %get-tuple-element.56), channel_id=1, source_target_pairs={{0,14},{2,0},{4,2},{6,4},{8,6},{10,8},{12,10},{14,12},{1,15},{3,1}... | collective-permute-start | bytes 589832 | tf_op jit(solution)/shard_map/ppermute | solution.py:298
  60.3 7.2 %collective-permute-start.7 = (f32[2,1,32,512]{3,2,1,0:T(8,128)S(1)}, f32[2,1,32,512]{3,2,1,0:T(8,128)S(1)}, u32[]{:S(2)}, u32[]{:S(2)}) collective-permute-start(f32[2,1,32,512]{3,2,1,0:T(8,128)S(1)} %get-tuple-element.52), channel_id=1, source_target_pairs={{0,14},{2,0},{4,2},{6,4},{8,6},{10,8},{12,10},{14,12},{1,15},{3,1}... | collective-permute-start | bytes 393224 | tf_op jit(solution)/shard_map/ppermute | solution.py:298

commit v5 on v3

--- a/solution.py
+++ b/solution.py
@@ -9,7 +9,7 @@
 LEVELS = 4
 HALO = 24
 LIMIT = 8 * 2**20
-STACK = 400
+STACK = 640
 STEPS = (
     ("y4", ()),
     ("b", ()),
@@ -22,7 +22,7 @@
     ("y1p", ("y3", "X", )),
     ("y7p", ("y5", )),
     ("y1q", ("y3", )),
-    ("y7q", ("y6", )),
+    ("y7q", ("y5", )),
     ("A", ()),
     ("B", ()),
     ("C", ()),
@@ -133,7 +133,6 @@
 
 
 FULL = ((2, 0), (0, 2), (1, 1), (1, 0), (0, 1), (0, 0))
-SHORT = ((1, 0), (0, 1), (0, 0))
 
 
 def y_kernel(count, places, starts, first_field, fields, spans, aliased):
@@ -182,8 +181,8 @@
         for start in range(0, len(units), together):
             group = units[start : start + together]
             middle = [stacked((0, LANES), t, group) for t in range(3)]
-            sides = [stacked((-LANES, UNIT), t, group) for t in range(2)]
-            solved = product(sides, outer, SHORT) + product(middle, inner, FULL)
+            sides = [stacked((-LANES, UNIT), t, group) for t in range(3)]
+            solved = product(sides, outer, FULL) + product(middle, inner, FULL)
             for number, (lane, at, first, last, _) in enumerate(group):
                 part = solved[number * size : (number + 1) * size]
                 result[:, 0, :, at : at + UNIT] = part.reshape(fields, rows, UNIT)
@@ -220,7 +219,7 @@
         input_output_aliases={len(operands): 0} if aliased else {},
         compiler_params=pltpu.CompilerParams(vmem_limit_bytes=LIMIT),
         cost_estimate=pl.CostEstimate(
-            flops=9 * 2 * 256 * size, bytes_accessed=8 * size, transcendentals=0
+            flops=12 * 2 * 256 * size, bytes_accessed=8 * size, transcendentals=0
         ),
     )(*[pltpu.with_memory_space_constraint(x, pltpu.VMEM) for x in operands], *([partial] if aliased else []))
 
@@ -279,6 +278,7 @@
     ring_2 = ((2 * c + e, 3 * c + e), (6 * c - e, 7 * c - e))
     ring_1 = ((7 * c - e, 8 * c + e), (9 * c - e, 10 * c + e))
     plans = {
+        "E": ([2, 3, 4, 5, 6, 0], ((2 * c + e, 7 * c - e), (8 * c + e, 9 * c - e)), ""),
         "A": ([3, 4, 5, 0], inner, ""),
         "B": ([2, 3, 5, 6], ring_2, ""),
         "C": ([6, 7, 0, 1, 2], ring_1, "p" if SPLIT else ""),

time: 68.3 us -> 70.4 us (1.031)
  waiting for transfers between devices: 24.7 us -> 25.8 us
  Pallas kernels: 15.9 us -> 16.7 us
    ppermute x9, waiting for transfers between devices: 24.6 us -> 25.8 us  [body(): lax.ppermute(cut, 'gy', [(i, (i + hop) % count) for i in range(count)])]
    pallas_call x4, Pallas kernels: 7.05 us -> 7.89 us  [y_call(): pl.pallas_call(y_kernel(count, places, starts, first_field, fields, spans...]
  transfers between devices with their start and end apart: 11 -> 11, of which waited for: 4 -> 3; matrix products, arithmetic and copies ran while one was open for 2% -> 2% of each run, Pallas kernels for 20% -> 20%
where the time goes in v5:
time: 70.4 us; the launch traced here: 70.2 us
  waiting for transfers between devices  25.8 us (37%)
  starting transfers between devices  25.6 us (36%)
  Pallas kernels  16.7 us (24%)
  local copies, waits for them, and re-layouts  1.15 us (2%)
  between operations  0.8 us (1%)
    ppermute x9, waiting for transfers between devices, body(): lax.ppermute(cut, 'gy', [(i, (i + hop) % count) for i in range(count)])  25.8 us
    ppermute x9, starting transfers between devices, body(): lax.ppermute(cut, 'gy', [(i, (i + hop) % count) for i in range(count)])  23.3 us
    pallas_call x4, Pallas kernels, y_call(): pl.pallas_call(y_kernel(count, places, starts, first_field, fields, spans...  7.89 us
    pallas_call x1, Pallas kernels, body(): pl.pallas_call(x_kernel, out_shape=jax.ShapeDtypeStruct(fields.shape, fie...  5.33 us
    pallas_call x3, Pallas kernels, body(): pl.pallas_call(cut_kernel(count, pieces), out_shape=[jax.ShapeDtypeStruct...  3.51 us
  transfers between devices with their start and end apart: 11, of which 3 were waited for; matrix products, arithmetic and copies ran while one was open for 2% of the time, Pallas kernels for 20%

profile of v5, /device:TPU:1, one launch (start us, length us, event | category | flops | bytes accessed | tf_op | source)
XLA Modules:
  0.0 70.2 jit_solution(7278139445530621309)
XLA Ops:
  0.6 1.0 %shard_map.86 = f32[5,1,32,512]{3,2,1,0:T(8,128)S(1)} custom-call(f32[5,1,256,512]{3,2,1,0:T(8,128)} %cells), custom_call_target="tpu_custom_call" | custom-call | bytes 655360 | tf_op jit(solution)/shard_map/pallas_call | solution.py:259
  1.6 0.0 copy-start
  1.6 7.8 %collective-permute-start.3 = (f32[5,1,32,512]{3,2,1,0:T(8,128)S(1)}, f32[5,1,32,512]{3,2,1,0:T(8,128)S(1)}, u32[]{:S(2)}, u32[]{:S(2)}) collective-permute-start(f32[5,1,32,512]{3,2,1,0:T(8,128)S(1)} %shard_map.86), channel_id=1, source_target_pairs={{0,8},{2,10},{4,12},{6,14},{8,0},{10,2},{12,4},{14,6},{1,9},{3,11}... | collective-permute-start | bytes 983048 | tf_op jit(solution)/shard_map/ppermute | solution.py:298
  9.5 1.1 %shard_map.87 = (f32[5,1,32,512]{3,2,1,0:T(8,128)S(1)}, f32[5,1,32,512]{3,2,1,0:T(8,128)S(1)}) custom-call(f32[5,1,256,512]{3,2,1,0:T(8,128)} %cells), custom_call_target="tpu_custom_call" | custom-call | bytes 1310720 | tf_op jit(solution)/shard_map/pallas_call | solution.py:259
  10.6 1.1 %fusion = (f32[5,1,24,512]{3,2,1,0:T(8,128)S(1)}, f32[5,1,24,512]{3,2,1,0:T(8,128)S(1)}) fusion(f32[5,1,256,512]{3,2,1,0:T(8,128)} %cells), kind=kLoop, calls=%fused_computation | loop fusion | bytes 983040 | tf_op jit(solution)/shard_map/slice | solution.py:303
  11.7 1.0 %collective-permute-start.2 = (f32[5,1,24,512]{3,2,1,0:T(8,128)S(1)}, f32[5,1,24,512]{3,2,1,0:T(8,128)S(1)}, u32[]{:S(2)}, u32[]{:S(2)}) collective-permute-start(f32[5,1,24,512]{3,2,1,0:T(8,128)S(1)} %get-tuple-element.60), channel_id=1, source_target_pairs={{16,0},{32,16},{48,32},{64,48},{80,64},{96,80},{112,96},{128,112},... | collective-permute-start | bytes 737288 | tf_op jit(solution)/shard_map/ppermute | solution.py:304
  12.7 1.3 %collective-permute-start.1 = (f32[5,1,24,512]{3,2,1,0:T(8,128)S(1)}, f32[5,1,24,512]{3,2,1,0:T(8,128)S(1)}, u32[]{:S(2)}, u32[]{:S(2)}) collective-permute-start(f32[5,1,24,512]{3,2,1,0:T(8,128)S(1)} %get-tuple-element.61), channel_id=1, source_target_pairs={{0,16},{16,32},{32,48},{48,64},{64,80},{80,96},{96,112},{112,128},... | collective-permute-start | bytes 737288 | tf_op jit(solution)/shard_map/ppermute | solution.py:301
  14.0 1.6 %collective-permute-start = (f32[5,1,32,512]{3,2,1,0:T(8,128)S(1)}, f32[5,1,32,512]{3,2,1,0:T(8,128)S(1)}, u32[]{:S(2)}, u32[]{:S(2)}) collective-permute-start(f32[5,1,32,512]{3,2,1,0:T(8,128)S(1)} %get-tuple-element.35), channel_id=1, source_target_pairs={{0,6},{2,8},{4,10},{6,12},{8,14},{10,0},{12,2},{14,4},{1,7},{3,9},... | collective-permute-start | bytes 983048 | tf_op jit(solution)/shard_map/ppermute | solution.py:298
  15.6 2.8 %collective-permute-start.6 = (f32[5,1,32,512]{3,2,1,0:T(8,128)S(1)}, f32[5,1,32,512]{3,2,1,0:T(8,128)S(1)}, u32[]{:S(2)}, u32[]{:S(2)}) collective-permute-start(f32[5,1,32,512]{3,2,1,0:T(8,128)S(1)} %get-tuple-element.48), channel_id=1, source_target_pairs={{0,10},{2,12},{4,14},{6,0},{8,2},{10,4},{12,6},{14,8},{1,11},{3,13... | collective-permute-start | bytes 983048 | tf_op jit(solution)/shard_map/ppermute | solution.py:298
  18.5 1.4 %shard_map.88 = (f32[5,1,32,512]{3,2,1,0:T(8,128)S(1)}, f32[5,1,32,512]{3,2,1,0:T(8,128)S(1)}, f32[3,1,32,512]{3,2,1,0:T(8,128)S(1)}, f32[3,1,32,512]{3,2,1,0:T(...) custom-call(f32[5,1,256,512]{3,2,1,0:T(8,128)} %cells), custom_call_target="tpu_custom_call" | custom-call | bytes 4587520 | tf_op jit(solution)/shard_map/pallas_call | solution.py:259
  19.9 0.0 collective-permute-done.3.refs_1_
  19.9 0.0 copy-start.1
  19.9 0.0 copy-start.2
  19.9 0.0 copy-start.3
  19.9 0.0 copy-start.4
  19.9 0.0 copy-start.5
  20.0 0.0 copy-start.6
  20.0 8.7 %collective-permute-start.8 = (f32[5,1,32,512]{3,2,1,0:T(8,128)S(1)}, f32[5,1,32,512]{3,2,1,0:T(8,128)S(1)}, u32[]{:S(2)}, u32[]{:S(2)}) collective-permute-start(f32[5,1,32,512]{3,2,1,0:T(8,128)S(1)} %get-tuple-element.54), channel_id=1, source_target_pairs={{0,12},{2,14},{4,0},{6,2},{8,4},{10,6},{12,8},{14,10},{1,13},{3,15... | collective-permute-start | bytes 983048 | tf_op jit(solution)/shard_map/ppermute | solution.py:298
  28.6 0.0 collective-permute-done.1.below
  28.6 0.9 %collective-permute-start.4 = (f32[5,1,32,512]{3,2,1,0:T(8,128)S(1)}, f32[5,1,32,512]{3,2,1,0:T(8,128)S(1)}, u32[]{:S(2)}, u32[]{:S(2)}) collective-permute-start(f32[5,1,32,512]{3,2,1,0:T(8,128)S(1)} %get-tuple-element.41), channel_id=1, source_target_pairs={{0,4},{2,6},{4,8},{6,10},{8,12},{10,14},{12,0},{14,2},{1,5},{3,7},... | collective-permute-start | bytes 983048 | tf_op jit(solution)/shard_map/ppermute | solution.py:298
  29.5 5.3 %shard_map.89 = f32[5,1,256,512]{3,2,1,0:T(8,128)} custom-call(f32[5,1,256,512]{3,2,1,0:T(8,128)S(1)} %copy-done, f32[5,1,24,512]{3,2,1,0:T(8,128)S(1)} %collective-permute-done.1.below, f32[5,1,24,512]{3,2,1,0:T(8,128)S(1)} %collective-permute-done.2.above), custom_call_target="tpu_custom_call" | custom-call | flops 13107200 | bytes 5242880 | tf_op jit(solution)/shard_map/pallas_call | solution.py:306
  34.9 15.6 %collective-permute-done.refs_2_ = f32[5,1,32,512]{3,2,1,0:T(8,128)S(1)} collective-permute-done((f32[5,1,32,512]{3,2,1,0:T(8,128)S(1)}, f32[5,1,32,512]{3,2,1,0:T(8,128)S(1)}, u32[]{:S(2)}, u32[]{:S(2)}) %collective-permute-start) | collective-permute-done | bytes 327712 | tf_op jit(solution)/shard_map/ppermute | solution.py:298
  50.5 0.0 collective-permute-done.6.refs_0_.refs_1_
  50.5 0.0 collective-permute-start.7
  50.5 0.0 collective-permute-start.10
  50.5 1.5 %collective-permute-start.9 = (f32[3,1,32,512]{3,2,1,0:T(8,128)S(1)}, f32[3,1,32,512]{3,2,1,0:T(8,128)S(1)}, u32[]{:S(2)}, u32[]{:S(2)}) collective-permute-start(f32[3,1,32,512]{3,2,1,0:T(8,128)S(1)} %get-tuple-element.55), channel_id=1, source_target_pairs={{0,2},{2,4},{4,6},{6,8},{8,10},{10,12},{12,14},{14,0},{1,3},{3,5},... | collective-permute-start | bytes 589832 | tf_op jit(solution)/shard_map/ppermute | solution.py:298
  52.0 2.6 %shard_map.90.refs_10_ = f32[5,1,32,4096]{3,2,1,0:T(8,128)} custom-call(f32[5,1,32,512]{3,2,1,0:T(8,128)S(1)} %collective-permute-done.6.refs_0_.refs_1_, f32[5,1,32,512]{3,2,1,0:T(8,128)S(1)} %collective-permute-done.3.refs_1_, f32[5,1,32,512]{3,2,1,0:T(8,128)S(1)} %collective-permute-done.refs_2_, f32[5,1,32,512]{3,2,1,0:T(8,128)S(1)} %get-tuple-element.45.refs_3_.refs_2_, ...), custom_call_target="tpu_custom_call" | custom-call | flops 1509949440 | bytes 1966080 | tf_op jit(solution)/shard_map/pallas_call | solution.py:210
  54.6 5.6 %collective-permute-done.8.refs_0_.refs_4_ = f32[5,1,32,512]{3,2,1,0:T(8,128)S(1)} collective-permute-done((f32[5,1,32,512]{3,2,1,0:T(8,128)S(1)}, f32[5,1,32,512]{3,2,1,0:T(8,128)S(1)}, u32[]{:S(2)}, u32[]{:S(2)}) %collective-permute-start.8) | collective-permute-done | bytes 327712 | tf_op jit(solution)/shard_map/ppermute | solution.py:298
  60.2 2.0 %shard_map.91.refs_11_ = f32[5,1,32,4096]{3,2,1,0:T(8,128)} custom-call(f32[5,1,32,512]{3,2,1,0:T(8,128)S(1)} %collective-permute-done.8.refs_0_.refs_4_, f32[5,1,32,512]{3,2,1,0:T(8,128)S(1)} %collective-permute-done.6.refs_0_.refs_1_, f32[5,1,32,512]{3,2,1,0:T(8,128)S(1)} %collective-permute-done.refs_2_, ...), custom_call_target="tpu_custom_call", output_to_operand_aliasing={{}: (10, {})} | custom-call | flops 1006632960 | bytes 1310720 | tf_op jit(solution)/shard_map/pallas_call | solution.py:210
  62.2 4.6 %collective-permute-done.10.refs_3_ = f32[3,1,32,512]{3,2,1,0:T(8,128)S(1)} collective-permute-done((f32[3,1,32,512]{3,2,1,0:T(8,128)S(1)}, f32[3,1,32,512]{3,2,1,0:T(8,128)S(1)}, u32[]{:S(2)}, u32[]{:S(2)}) %collective-permute-start.10) | collective-permute-done | bytes 196640 | tf_op jit(solution)/shard_map/ppermute | solution.py:298
  66.8 1.8 %shard_map.92.refs_11_ = f32[5,1,32,4096]{3,2,1,0:T(8,128)} custom-call(f32[5,1,32,512]{3,2,1,0:T(8,128)S(1)} %collective-permute-done.4.refs_3_.refs_0_, f32[3,1,32,512]{3,2,1,0:T(8,128)S(1)} %collective-permute-done.9.refs_1_, f32[5,1,32,512]{3,2,1,0:T(8,128)S(1)} %get-tuple-element.45.refs_3_.refs_2_, ...), custom_call_target="tpu_custom_call", output_to_operand_aliasing={{}: (11, {})} | custom-call | flops 905969664 | bytes 1179648 | tf_op jit(solution)/shard_map/pallas_call | solution.py:210
  68.7 1.5 %shard_map.93 = f32[5,1,32,4096]{3,2,1,0:T(8,128)} custom-call(f32[5,1,32,512]{3,2,1,0:T(8,128)S(1)} %collective-permute-done.4.refs_3_.refs_0_, f32[2,1,32,512]{3,2,1,0:T(8,128)S(1)} %collective-permute-done.5.refs_1_, f32[5,1,32,512]{3,2,1,0:T(8,128)S(1)} %get-tuple-element.45.refs_3_.refs_2_, ...), custom_call_target="tpu_custom_call", output_to_operand_aliasing={{}: (11, {})} | custom-call | flops 603979776 | bytes 786432 | tf_op jit(solution)/shard_map/pallas_call | solution.py:210
  (13 shorter events, 0.0 us)
Async XLA Ops:
  1.6 27.9 %copy-start = (f32[5,1,256,512]{3,2,1,0:T(8,128)S(1)}, f32[5,1,256,512]{3,2,1,0:T(8,128)}, u32[]{:S(2)}) copy-start(f32[5,1,256,512]{3,2,1,0:T(8,128)} %cells) | copy-start | bytes 7864324
  1.6 18.2 %collective-permute-start.3 = (f32[5,1,32,512]{3,2,1,0:T(8,128)S(1)}, f32[5,1,32,512]{3,2,1,0:T(8,128)S(1)}, u32[]{:S(2)}, u32[]{:S(2)}) collective-permute-start(f32[5,1,32,512]{3,2,1,0:T(8,128)S(1)} %shard_map.86), channel_id=1, source_target_pairs={{0,8},{2,10},{4,12},{6,14},{8,0},{10,2},{12,4},{14,6},{1,9},{3,11}... | collective-permute-start | bytes 983048 | tf_op jit(solution)/shard_map/ppermute | solution.py:298
  11.7 8.3 %collective-permute-start.2 = (f32[5,1,24,512]{3,2,1,0:T(8,128)S(1)}, f32[5,1,24,512]{3,2,1,0:T(8,128)S(1)}, u32[]{:S(2)}, u32[]{:S(2)}) collective-permute-start(f32[5,1,24,512]{3,2,1,0:T(8,128)S(1)} %get-tuple-element.60), channel_id=1, source_target_pairs={{16,0},{32,16},{48,32},{64,48},{80,64},{96,80},{112,96},{128,112},... | collective-permute-start | bytes 737288 | tf_op jit(solution)/shard_map/ppermute | solution.py:304
  12.7 15.9 %collective-permute-start.1 = (f32[5,1,24,512]{3,2,1,0:T(8,128)S(1)}, f32[5,1,24,512]{3,2,1,0:T(8,128)S(1)}, u32[]{:S(2)}, u32[]{:S(2)}) collective-permute-start(f32[5,1,24,512]{3,2,1,0:T(8,128)S(1)} %get-tuple-element.61), channel_id=1, source_target_pairs={{0,16},{16,32},{32,48},{48,64},{64,80},{80,96},{96,112},{112,128},... | collective-permute-start | bytes 737288 | tf_op jit(solution)/shard_map/ppermute | solution.py:301
  14.0 36.5 %collective-permute-start = (f32[5,1,32,512]{3,2,1,0:T(8,128)S(1)}, f32[5,1,32,512]{3,2,1,0:T(8,128)S(1)}, u32[]{:S(2)}, u32[]{:S(2)}) collective-permute-start(f32[5,1,32,512]{3,2,1,0:T(8,128)S(1)} %get-tuple-element.35), channel_id=1, source_target_pairs={{0,6},{2,8},{4,10},{6,12},{8,14},{10,0},{12,2},{14,4},{1,7},{3,9},... | collective-permute-start | bytes 983048 | tf_op jit(solution)/shard_map/ppermute | solution.py:298
  15.6 34.9 %collective-permute-start.6 = (f32[5,1,32,512]{3,2,1,0:T(8,128)S(1)}, f32[5,1,32,512]{3,2,1,0:T(8,128)S(1)}, u32[]{:S(2)}, u32[]{:S(2)}) collective-permute-start(f32[5,1,32,512]{3,2,1,0:T(8,128)S(1)} %get-tuple-element.48), channel_id=1, source_target_pairs={{0,10},{2,12},{4,14},{6,0},{8,2},{10,4},{12,6},{14,8},{1,11},{3,13... | collective-permute-start | bytes 983048 | tf_op jit(solution)/shard_map/ppermute | solution.py:298
  19.9 32.1 %copy-start.1 = (bf16[256,256]{1,0:T(8,128)(2,1)S(1)}, bf16[256,256]{1,0:T(8,128)(2,1)}, u32[]{:S(2)}) copy-start(bf16[256,256]{1,0:T(8,128)(2,1)} %constant.17.clone.refs_9_.refs_10_) | copy-start | bytes 393220
  19.9 32.1 %copy-start.2 = (bf16[256,256]{1,0:T(8,128)(2,1)S(1)}, bf16[256,256]{1,0:T(8,128)(2,1)}, u32[]{:S(2)}) copy-start(bf16[256,256]{1,0:T(8,128)(2,1)} %constant.16.clone.refs_8_.refs_9_) | copy-start | bytes 393220
  19.9 32.1 %copy-start.3 = (bf16[256,256]{1,0:T(8,128)(2,1)S(1)}, bf16[256,256]{1,0:T(8,128)(2,1)}, u32[]{:S(2)}) copy-start(bf16[256,256]{1,0:T(8,128)(2,1)} %constant.15.clone.refs_7_.refs_8_) | copy-start | bytes 393220
  19.9 32.1 %copy-start.4 = (bf16[256,256]{1,0:T(8,128)(2,1)S(1)}, bf16[256,256]{1,0:T(8,128)(2,1)}, u32[]{:S(2)}) copy-start(bf16[256,256]{1,0:T(8,128)(2,1)} %constant.14.clone.refs_6_.refs_7_) | copy-start | bytes 393220
  19.9 32.1 %copy-start.5 = (bf16[256,256]{1,0:T(8,128)(2,1)S(1)}, bf16[256,256]{1,0:T(8,128)(2,1)}, u32[]{:S(2)}) copy-start(bf16[256,256]{1,0:T(8,128)(2,1)} %constant.13.clone.refs_5_.refs_6_) | copy-start | bytes 393220
  20.0 32.1 %copy-start.6 = (bf16[256,256]{1,0:T(8,128)(2,1)S(1)}, bf16[256,256]{1,0:T(8,128)(2,1)}, u32[]{:S(2)}) copy-start(bf16[256,256]{1,0:T(8,128)(2,1)} %constant.12.clone.refs_4_.refs_5_) | copy-start | bytes 393220
  20.0 40.2 %collective-permute-start.8 = (f32[5,1,32,512]{3,2,1,0:T(8,128)S(1)}, f32[5,1,32,512]{3,2,1,0:T(8,128)S(1)}, u32[]{:S(2)}, u32[]{:S(2)}) collective-permute-start(f32[5,1,32,512]{3,2,1,0:T(8,128)S(1)} %get-tuple-element.54), channel_id=1, source_target_pairs={{0,12},{2,14},{4,0},{6,2},{8,4},{10,6},{12,8},{14,10},{1,13},{3,15... | collective-permute-start | bytes 983048 | tf_op jit(solution)/shard_map/ppermute | solution.py:298
  28.6 31.6 %collective-permute-start.4 = (f32[5,1,32,512]{3,2,1,0:T(8,128)S(1)}, f32[5,1,32,512]{3,2,1,0:T(8,128)S(1)}, u32[]{:S(2)}, u32[]{:S(2)}) collective-permute-start(f32[5,1,32,512]{3,2,1,0:T(8,128)S(1)} %get-tuple-element.41), channel_id=1, source_target_pairs={{0,4},{2,6},{4,8},{6,10},{8,12},{10,14},{12,0},{14,2},{1,5},{3,7},... | collective-permute-start | bytes 983048 | tf_op jit(solution)/shard_map/ppermute | solution.py:298
  50.5 18.2 %collective-permute-start.7 = (f32[2,1,32,512]{3,2,1,0:T(8,128)S(1)}, f32[2,1,32,512]{3,2,1,0:T(8,128)S(1)}, u32[]{:S(2)}, u32[]{:S(2)}) collective-permute-start(f32[2,1,32,512]{3,2,1,0:T(8,128)S(1)} %get-tuple-element.50), channel_id=1, source_target_pairs={{0,14},{2,0},{4,2},{6,4},{8,6},{10,8},{12,10},{14,12},{1,15},{3,1}... | collective-permute-start | bytes 393224 | tf_op jit(solution)/shard_map/ppermute | solution.py:298
  50.5 16.3 %collective-permute-start.10 = (f32[3,1,32,512]{3,2,1,0:T(8,128)S(1)}, f32[3,1,32,512]{3,2,1,0:T(8,128)S(1)}, u32[]{:S(2)}, u32[]{:S(2)}) collective-permute-start(f32[3,1,32,512]{3,2,1,0:T(8,128)S(1)} %get-tuple-element.56), channel_id=1, source_target_pairs={{0,14},{2,0},{4,2},{6,4},{8,6},{10,8},{12,10},{14,12},{1,15},{3,1}... | collective-permute-start | bytes 589832 | tf_op jit(solution)/shard_map/ppermute | solution.py:298
  50.5 16.3 %collective-permute-start.9 = (f32[3,1,32,512]{3,2,1,0:T(8,128)S(1)}, f32[3,1,32,512]{3,2,1,0:T(8,128)S(1)}, u32[]{:S(2)}, u32[]{:S(2)}) collective-permute-start(f32[3,1,32,512]{3,2,1,0:T(8,128)S(1)} %get-tuple-element.55), channel_id=1, source_target_pairs={{0,2},{2,4},{4,6},{6,8},{8,10},{10,12},{12,14},{14,0},{1,3},{3,5},... | collective-permute-start | bytes 589832 | tf_op jit(solution)/shard_map/ppermute | solution.py:298
  60.2 8.4 %collective-permute-start.5 = (f32[2,1,32,512]{3,2,1,0:T(8,128)S(1)}, f32[2,1,32,512]{3,2,1,0:T(8,128)S(1)}, u32[]{:S(2)}, u32[]{:S(2)}) collective-permute-start(f32[2,1,32,512]{3,2,1,0:T(8,128)S(1)} %get-tuple-element.44), channel_id=1, source_target_pairs={{0,2},{2,4},{4,6},{6,8},{8,10},{10,12},{12,14},{14,0},{1,3},{3,5},... | collective-permute-start | bytes 393224 | tf_op jit(solution)/shard_map/ppermute | solution.py:298
